TPU v7x, 128 devices: a whole 4x4x4 slice. The times are simulated.
128 devices in a mesh: seq: 8 (over y, core), tp: 16 (over x, z).
Axes of the slice: x: 4, y: 4, z: 4, core: 2. Of those that a mesh axis runs over, the one named last changes fastest.
Arguments:
- queries: bfloat16 [64, 8, 16, 128], P('tp'), may hold values from -10 to 10
- cache_kv: bfloat16 [64, 8, 2048, 256], P('tp', None, 'seq'), may hold values from -5 to 5
- new_kv: bfloat16 [64, 8, 256, 256], P('tp', None, 'seq'), may hold values from -5 to 5
- ctx_len: int32 [64], replicated, may hold values from 2 to 2048, as said below
- new_len: int32 [64], replicated, may hold values from 1 to 256, as said below
- owner: int32 [64], replicated, may hold values from 0 to 7, as said below
- wo: bfloat16 [16384, 16384], P(('seq', 'tp')), may hold values from -1 to 1
- hidden_in: bfloat16 [64, 16384], P(None, ('seq', 'tp')), may hold values from -3 to 3
- norm_gain: float32 [16384], P(('seq', 'tp')), may hold values from 0.5 to 1.5
Outputs:
- residual_out: bfloat16 [64, 16384], P(None, ('seq', 'tp'))
- normed: bfloat16 [64, 16384], P(None, ('seq', 'tp'))
- appended: bfloat16 [64, 8, 2048, 256], P('tp', None, 'seq')
Inputs may be any that keep to these rules, and one draw needn't show every extreme that they name: `ctx_len`: some request reaches 2048. `new_len`: some request reaches 256. `owner`: every shard owns some request.
All inputs are finite; a program needn't handle non-finite values.
Results may differ from a plain program's by a relative error of at most 0.014.
Values may be sent and summed in bfloat16 or wider, within the bound.
A program may use at most 64 MiB of HBM per device.

v0:
```python
import jax
import jax.numpy as jnp
from jax import lax
from jax.sharding import PartitionSpec as P

D = 16384
HD = 128


def joined(x, axis, combine):
    everything = jax.tree.map(
        lambda part, kind: lax.all_gather(part.astype(kind), axis),
        x,
        (jnp.bfloat16, jnp.bfloat16, jnp.bfloat16),
    )

    def take(k):
        return jax.tree.map(lambda part, own: part[k].astype(own.dtype), everything, x)

    return lax.fori_loop(
        1, lax.axis_size(axis), lambda k, so_far: combine(so_far, take(k)), take(0)
    )


def combine_parts(first, second):
    top = jnp.maximum(first[0], second[0])
    scale_one = jnp.exp(first[0] - top)
    scale_two = jnp.exp(second[0] - top)
    total = first[1] * scale_one + second[1] * scale_two
    weighted = first[2] * scale_one[..., None] + second[2] * scale_two[..., None]
    return (top, total, weighted)


def attend(queries, block, valid):
    keys = block[:, :, :, :HD]
    values = block[:, :, :, HD:]
    scores = jnp.einsum(
        "rhgd,rhpd->rhgp", queries, keys, preferred_element_type=jnp.float32
    ) * HD ** (-0.5)
    mask = valid[:, None, None, :]
    top = jnp.max(jnp.where(mask, scores, -1e30), axis=-1)
    weights = jnp.where(mask, jnp.exp(scores - top[..., None]), 0.0)
    total = jnp.sum(weights, axis=-1)
    weighted = jnp.einsum("rhgp,rhpd->rhgd", weights, values.astype(jnp.float32))
    return (top, total, weighted)


def per_device(queries, cache_kv, new_kv, ctx_len, new_len, owner, wo, hidden_in, norm_gain):
    req_rows = queries.shape[0]
    cache_width = cache_kv.shape[2]
    seq_count = lax.axis_size("seq")
    seq_index = lax.axis_index("seq")
    tp_index = lax.axis_index("tp")
    my_ctx = lax.dynamic_slice_in_dim(ctx_len, tp_index * req_rows, req_rows)
    my_new = lax.dynamic_slice_in_dim(new_len, tp_index * req_rows, req_rows)
    my_owner = lax.dynamic_slice_in_dim(owner, tp_index * req_rows, req_rows)
    delivered = lax.all_gather(new_kv, "seq", axis=2, tiled=True)
    block_width = delivered.shape[2]
    block_slots = jnp.arange(block_width, dtype=jnp.int32)
    owned = my_owner == seq_index
    kept = owned[:, None] & (block_slots[None, :] < my_new[:, None])
    appended = jnp.where(kept[:, None, :, None], delivered, jnp.zeros((), jnp.bfloat16))
    cache_pos = seq_index * cache_width + jnp.arange(cache_width, dtype=jnp.int32)
    cache_part = attend(queries, cache_kv, cache_pos[None, :] < my_ctx[:, None])
    new_part = attend(queries, delivered, kept)
    top, total, weighted = combine_parts(cache_part, new_part)
    heads = top.shape[1] * top.shape[2]
    top = top.reshape(req_rows, heads)
    total = total.reshape(req_rows, heads)
    weighted = weighted.reshape(req_rows, heads, HD)
    kept_heads = heads // seq_count
    top, total, weighted = joined((top, total, weighted), "seq", combine_parts)
    context = (weighted / total[..., None]).astype(jnp.bfloat16)
    context = lax.dynamic_slice_in_dim(context, seq_index * kept_heads, kept_heads, 1)
    relaid = lax.all_to_all(context, "tp", split_axis=1, concat_axis=0, tiled=True)
    batch = relaid.shape[0]
    flat = relaid.reshape(batch, relaid.shape[1] * HD)
    summed = lax.psum_scatter(
        lax.dot_general(wo, flat, (((0,), (1,)), ((), ())), preferred_element_type=jnp.float32),
        ("seq", "tp"),
        scatter_dimension=0,
        tiled=True,
    )
    stream = hidden_in.astype(jnp.float32) + summed.T
    residual_out = stream.astype(jnp.bfloat16)
    squares = lax.psum(jnp.sum(stream * stream, axis=1), ("seq", "tp"))
    scale = lax.rsqrt(squares / D + 1e-05)
    normed = (stream * scale[:, None] * norm_gain[None, :]).astype(jnp.bfloat16)
    return (residual_out, normed, appended)


def solution(mesh):
    in_specs = (
        P("tp", None, None, None),
        P("tp", None, "seq", None),
        P("tp", None, "seq", None),
        P(),
        P(),
        P(),
        P(("seq", "tp"), None),
        P(None, ("seq", "tp")),
        P(("seq", "tp")),
    )
    out_specs = (P(None, ("seq", "tp")), P(None, ("seq", "tp")), P("tp", None, "seq", None))
    return jax.shard_map(
        per_device, mesh=mesh, in_specs=in_specs, out_specs=out_specs, check_vma=False
    )
```

profile of v0, /device:TPU:1, one launch (start us, length us, event | category | flops | bytes accessed | tf_op | source)
XLA Modules:
  0.0 814.7 jit_solution(8883907987833329009)
XLA Ops:
  7.2 0.0 copy-start
  7.2 0.0 all-gather.3.cloned.1.call-start
  7.2 0.7 all-gather.3.cloned.1.call-update
  7.9 0.0 all-gather.5.cloned.1.call-start
  8.0 0.7 dynamic_slice.44
  8.7 0.7 dynamic_slice.42
  9.4 0.7 dynamic-slice_compare_fusion
  10.2 0.1 fusion.42
  10.2 0.1 broadcast_compare_fusion
  10.3 0.0 copy-done
  10.3 2.3 select_reduce_fusion.1
  12.6 32.9 %all-gather.3.cloned.1.call-done = bf16[4,8,256,256]{3,2,1,0:T(8,128)(2,1)} async-done(((bf16[4,8,32,256]{3,2,1,0:T(8,128)(2,1)}), bf16[4,8,256,256]{3,2,1,0:T(8,128)(2,1)}) %all-gather.3.cloned.1.call-update) | async-done | bytes 4194320 | tf_op jit(solution)/shard_map/all_gather | solution.py:57
  45.5 0.0 copy-start.1
  45.5 2.5 select_reduce_fusion
  48.0 2.0 fusion.23
  50.0 0.0 copy-done.1
  50.0 1.1 fusion.26
  51.2 0.0 all-gather.5.cloned.1.call-update
  51.2 0.0 reduce-scatter.2.cloned.1.call-start
  51.3 0.1 reduce_max.23
  51.3 0.3 fusion.29
  51.6 0.1 reduce_sum.32
  51.7 0.1 reduce_max.25
  51.8 0.3 fusion.30
  52.1 0.1 reduce_sum.34
  52.2 8.7 %all_gather.17 = bf16[8,4,128]{2,1,0:T(4,128)(2,1)S(1)} all-gather(bf16[1,4,128]{2,1,0:T(4,128)(2,1)S(1)} %add_convert_fusion), channel_id=1, replica_groups=mesh['seq'=8,'tp'=16] {'seq'}, dimensions={0}, use_global_device_ids=true | all-gather | bytes 9216 | tf_op jit(solution)/shard_map/all_gather | solution.py:12
  60.9 9.0 %all_gather.16 = bf16[8,4,128]{2,1,0:T(4,128)(2,1)S(1)} all-gather(bf16[1,4,128]{2,1,0:T(4,128)(2,1)S(1)} %max.46), channel_id=1, replica_groups=mesh['seq'=8,'tp'=16] {'seq'}, dimensions={0}, use_global_device_ids=true | all-gather | bytes 9216 | tf_op jit(solution)/shard_map/all_gather | solution.py:12
  69.8 4.9 all-gather.5.cloned.1.call-done
  74.7 0.9 fusion.37
  75.6 8.7 %while.19 = (s32[]{:T(128)}, f32[4,128]{1,0:T(4,128)S(1)}, f32[4,128]{1,0:T(4,128)S(1)}, f32[4,128,128]{2,1,0:T(8,128)S(1)}, bf16[8,4,128]{2,1,0:T(4,128)(2,1)S(...) while((s32[]{:T(128)}, f32[4,128]{1,0:T(4,128)S(1)}, ...), condition=%wide.region_5.6_spmd, body=%wide.region_4.5_spmd.sunk | while | flops 266245 | bytes 673943 | solution.py:20
  75.7 1.2 fusion.55
  76.9 1.2 fusion.55
  78.1 1.2 fusion.55
  79.4 1.2 fusion.55
  80.6 1.2 fusion.55
  81.9 1.2 fusion.55
  83.1 1.2 fusion.55
  84.3 0.2 copy.14
  84.5 0.1 copy.13
  84.6 0.1 fusion.38
  84.7 12.9 %all_to_all.15 = bf16[4,16,128]{2,0,1:T(4,128)(2,1)S(1)} all-to-all(bf16[4,16,128]{2,0,1:T(4,128)(2,1)S(1)} %fusion.38), channel_id=1, replica_groups=mesh['seq'=8,'tp'=16] {'tp'}, dimensions={1} | all-to-all | bytes 32768 | tf_op jit(solution)/shard_map/all_to_all | solution.py:75
  97.6 4.9 convolution_bitcast_fusion
  102.5 0.0 reduce-scatter.2.cloned.1.call-update
  102.5 0.0 copy-start.2
  102.5 0.0 copy-start.3
  102.5 4.6 broadcast_select_fusion
  107.1 605.2 %reduce-scatter.2.cloned.1.call-done = f32[128,64]{0,1:T(8,128)} async-done(((f32[16384,64]{0,1:T(8,128)}), f32[128,64]{0,1:T(8,128)}) %reduce-scatter.2.cloned.1.call-update) | async-done | bytes 32784 | tf_op jit(solution)/shard_map/reduce_scatter | solution.py:78
  712.3 0.0 copy-done.2
  712.3 0.9 multiply_reduce_fusion
  713.2 93.5 %psum.7 = f32[64]{0:T(128)S(1)} all-reduce(f32[64]{0:T(128)S(1)} %multiply_reduce_fusion), channel_id=1, replica_groups=mesh['seq'=8,'tp'=16] {'seq','tp'}, use_global_device_ids=true, to_apply=%region_8.9 | all-reduce | flops 64 | bytes 512 | tf_op jit(solution)/shard_map/psum | solution.py:86
  806.7 0.0 copy-done.3
  806.7 1.4 multiply_convert_fusion
  (15 shorter events, 0.3 us)
Async XLA Ops:
  7.2 3.1 copy-start
  7.2 38.3 %all-gather.3.cloned.1.call-start = ((), (), s32[]{:S(2)}) async-start(), calls=%async_computation.2 | async-start | bytes 4718592 | tf_op jit(solution)/shard_map/all_gather | solution.py:57
  7.9 66.8 %all-gather.5.cloned.1.call-start = ((), (), s32[]{:S(2)}) async-start(), calls=%async_computation.3 | async-start | bytes 1179648 | tf_op jit(solution)/shard_map/all_gather | solution.py:12
  45.5 4.5 copy-start.1
  51.2 661.1 %reduce-scatter.2.cloned.1.call-start = ((), (), s32[]{:S(2)}) async-start(), calls=%async_computation.4 | async-start | bytes 4227072 | tf_op jit(solution)/shard_map/reduce_scatter | solution.py:78
  102.5 609.8 %copy-start.2 = (bf16[64,128]{1,0:T(8,128)(2,1)S(1)}, bf16[64,128]{1,0:T(8,128)(2,1)}, u32[]{:S(2)}) copy-start(bf16[64,128]{1,0:T(8,128)(2,1)} %param.18) | copy-start | bytes 49156
  102.5 704.2 %copy-start.3 = (f32[128]{0:T(128)S(1)}, f32[128]{0:T(128)}, u32[]{:S(2)}) copy-start(f32[128]{0:T(128)} %param.19) | copy-start | bytes 1540
Sparse Core Ops, SparseCore 0:
  9.7 35.7 all-gather.2
  51.3 23.3 all-gather.4
  102.6 609.6 reduce-scatter.1
where the time goes:
time: 815 us
  waiting for transfers between devices  644 us (79%)
  blocking collectives  124 us (15%)
  other arithmetic  17.9 us (2%)
  between operations  13.9 us (2%)
  matrix products  12.8 us (2%)
    reduce_scatter x1, waiting for transfers between devices, per_device(): lax.psum_scatter(lax.dot_general(wo, flat, (((0,), (1,)), ((), ())), pref...  605 us
    psum x1, blocking collectives, per_device(): squares = lax.psum(jnp.sum(stream * stream, axis=1), ('seq', 'tp'))  93.5 us
    all_gather x1, waiting for transfers between devices, per_device(): delivered = lax.all_gather(new_kv, 'seq', axis=2, tiled=True)  32.9 us
    all_gather x2, blocking collectives, joined(): lax.all_gather(part.astype(kind), axis)  17.7 us
  transfers between devices with their start and end apart: 3, of which 3 were waited for; matrix products, arithmetic and copies ran while one was open for 1% of the time, Pallas kernels for 0%

commit v1 on v0

v1 whole, which is shorter than its diff:
```python
import functools

import jax
import jax.numpy as jnp
from jax import lax
from jax.experimental import pallas as pl
from jax.experimental.pallas import tpu as pltpu
from jax.sharding import PartitionSpec as P

D = 16384
HD = 128
KVH = 8
GROUP = 16
REQ = 4
WIDTH = 256
SHARE = 32
KEYS = WIDTH + SHARE
NEG = -1e30
MESH = pl.DeviceIdType.MESH


def remote(src, dst, send, recv, device):
    return pltpu.make_async_remote_copy(
        src_ref=src, dst_ref=dst, send_sem=send, recv_sem=recv, device_id=device, device_id_type=MESH
    )


def kernel(
    ctx_ref, new_ref, q_hbm, cache_hbm, newkv_hbm, wo_hbm, hidden_hbm, gain_hbm,
    res_ref, norm_ref, deliv_hbm,
    q_v, kv, w_v, hid_v, gain_v,
    osend, orecv, lsend, lrecv, csend, crecv,
    a_send, b_send, a_recv, b_recv, a2_send, b2_send, a2_recv, b2_recv,
    y_send, y_recv, n_send, n_recv, m_send, m_recv, rows_v,
    loc_sem, kv_sem, wl_sem, ws_sem, wr_sem,
    os_sem, or_sem, ls_sem, lr_sem, cs_sem, cr_sem,
    r1s_sem, r1r_sem, r2s_sem, r2r_sem, ys_sem, yr_sem,
    ns_sem, nr_sem, ms_sem, mr_sem,
    gs_sem, gr_sem, ps_sem, pr_sem, gl_sem,
):
    s = lax.axis_index("seq")
    t = lax.axis_index("tp")
    y, c = s // 2, s % 2
    x, z = t // 4, t % 4
    sp = y * 2 + (1 - c)

    def seq_peer(i):
        return lax.rem(s + 1 + i, 8)

    def tp_peer(i):
        return lax.rem(t + 1 + i, 16)

    def y_at(d):
        return lax.rem(y + d, 4) * 2 + c

    def x_at(d):
        return lax.rem(x + d, 4) * 4 + z

    def z_at(d):
        return x * 4 + lax.rem(z + d, 4)

    barrier = pltpu.get_barrier_semaphore()

    def greet_seq(i, _):
        pl.semaphore_signal(barrier, inc=1, device_id=(seq_peer(i), t), device_id_type=MESH)
        return 0

    def greet_tp(i, _):
        pl.semaphore_signal(barrier, inc=1, device_id=(s, tp_peer(i)), device_id_type=MESH)
        pl.semaphore_signal(barrier, inc=1, device_id=(sp, tp_peer(i)), device_id_type=MESH)
        return 0

    lax.fori_loop(0, 7, greet_seq, 0)
    lax.fori_loop(0, 15, greet_tp, 0)

    q_copy = pltpu.make_async_copy(q_hbm, q_v, loc_sem.at[0])
    h_copy = pltpu.make_async_copy(hidden_hbm, hid_v, loc_sem.at[1])
    g_copy = pltpu.make_async_copy(gain_hbm, gain_v, loc_sem.at[2])
    q_copy.start()

    def kv_copies(r):
        return (
            pltpu.make_async_copy(cache_hbm.at[r], kv.at[r, :, pl.ds(0, WIDTH), :], kv_sem.at[r, 0]),
            pltpu.make_async_copy(newkv_hbm.at[r], kv.at[r, :, pl.ds(WIDTH, SHARE), :], kv_sem.at[r, 1]),
        )

    for r in range(REQ):
        for copy in kv_copies(r):
            copy.start()
    h_copy.start()
    g_copy.start()

    def w_local(j):
        return pltpu.make_async_copy(
            wo_hbm.at[:, pl.ds(pl.multiple_of(j * 4096 + c * 2048, 2048), 2048)],
            w_v.at[j, pl.ds(pl.multiple_of(c * 128, 128), 128), :],
            wl_sem.at[j],
        )

    def w_remote(j):
        return remote(
            wo_hbm.at[:, pl.ds(pl.multiple_of(j * 4096 + (1 - c) * 2048, 2048), 2048)],
            w_v.at[j, pl.ds(pl.multiple_of(c * 128, 128), 128), :],
            ws_sem.at[j], wr_sem.at[j], (sp, t),
        )

    for j in range(4):
        w_local(j).start()

    def block(half, who):
        return deliv_hbm.at[pl.ds(half * 2, 2), :, pl.ds(pl.multiple_of(who * SHARE, SHARE), SHARE), :]

    own = [
        pltpu.make_async_copy(newkv_hbm.at[pl.ds(half * 2, 2)], block(half, s), gl_sem.at[half])
        for half in range(2)
    ]

    def ring(way, slot, src, dst):
        return remote(src, dst, gs_sem.at[way, slot], gr_sem.at[way, slot], (y_at(1 if way == 0 else 3), t))

    def first(way, order):
        half = order if way == 0 else 1 - order
        return ring(way, order, newkv_hbm.at[pl.ds(half * 2, 2)], block(half, s))

    def second(way):
        who = y_at(3) if way == 0 else y_at(1)
        return ring(way, 2, block(way, who), block(way, who))

    def pair(slot, src, half, who):
        return remote(src, block(half, who), ps_sem.at[slot], pr_sem.at[slot], (sp, t))

    def pair_own(half):
        return pair(half, newkv_hbm.at[pl.ds(half * 2, 2)], half, s)

    def pair_near(way, order):
        half = order if way == 0 else 1 - order
        who = y_at(3) if way == 0 else y_at(1)
        return pair(2 + way * 2 + order, block(half, who), half, who)

    def pair_far(way):
        return pair(6 + way, block(way, y_at(2)), way, y_at(2))

    pl.semaphore_wait(barrier, 37)

    for order in range(2):
        for way in range(2):
            first(way, order).start()
    for j in range(4):
        w_remote(j).start()
    for half in range(2):
        own[half].start()
        pair_own(half).start()

    q_copy.wait()
    col = lax.broadcasted_iota(jnp.int32, (GROUP, KEYS), 1)
    lane = lax.broadcasted_iota(jnp.int32, (GROUP, 128), 1)

    def attend(r, ls):
        for copy in kv_copies(r):
            copy.wait()
        live_ctx = jnp.minimum(ctx_ref[t * REQ + r] - s * WIDTH, WIDTH)
        live_new = new_ref[t * REQ + r] - s * SHARE + WIDTH
        mask = (col < live_ctx) | ((col >= WIDTH) & (col < live_new))
        for h in range(KVH):
            scores = lax.dot_general(
                q_v[r, h], kv[r, h, :, :HD], (((1,), (1,)), ((), ())), preferred_element_type=jnp.float32
            ) * HD ** (-0.5)
            scores = jnp.where(mask, scores, NEG)
            top = jnp.max(scores, axis=1, keepdims=True)
            weights = jnp.where(mask, jnp.exp(scores - top), 0.0)
            total = jnp.maximum(jnp.sum(weights, axis=1, keepdims=True), 1e-30)
            out = jnp.dot(weights.astype(jnp.bfloat16), kv[r, h, :, HD:], preferred_element_type=jnp.float32)
            osend[h, pl.ds(pl.multiple_of(r * GROUP, GROUP), GROUP), :] = (out / total).astype(jnp.bfloat16)
            ls = jnp.where(lane == h * REQ + r, top + jnp.log(total), ls)
        return ls

    lsend[...] = lax.fori_loop(0, REQ, attend, jnp.zeros((GROUP, 128), jnp.float32))

    def o_copy(k, slot):
        return remote(osend.at[k], orecv.at[slot], os_sem.at[k], or_sem.at[slot], (k, t))

    def l_copy(k, slot):
        return remote(lsend, lrecv.at[slot], ls_sem.at[k], lr_sem.at[slot], (k, t))

    def send_o(i, _):
        k = seq_peer(i)
        l_copy(k, s).start()
        o_copy(k, s).start()
        return 0

    lax.fori_loop(0, 7, send_o, 0)
    orecv[s] = osend[s]
    lrecv[s] = lsend[...]

    def wait_o(i, _):
        k = seq_peer(i)
        l_copy(k, k).wait_recv()
        o_copy(k, k).wait_recv()
        return 0

    lax.fori_loop(0, 7, wait_o, 0)
    shift = lax.rem(128 - s * REQ, 128)
    tops = [lrecv[k] for k in range(8)]
    top = functools.reduce(jnp.maximum, tops)
    exps = [jnp.exp(v - top) for v in tops]
    total = functools.reduce(jnp.add, exps)
    shares = [pltpu.roll(e / total, shift, 1) for e in exps]
    for r in range(REQ):
        context = jnp.zeros((GROUP, HD), jnp.float32)
        for k in range(8):
            part = orecv[k, r * GROUP:(r + 1) * GROUP, :].astype(jnp.float32)
            context = context + part * shares[k][:, r:r + 1]
        csend[pl.ds(r, GROUP, stride=8), :] = context
        csend[pl.ds(r + REQ, GROUP, stride=8), :] = context

    def c_copy(core, g, slot_core, slot_t):
        return remote(
            csend.at[pl.ds(pl.multiple_of(g * 8, 8), 8), :],
            crecv.at[slot_core, pl.ds(pl.multiple_of(slot_t * 8, 8), 8), :],
            cs_sem.at[core, g], cr_sem.at[slot_core, slot_t],
            (y * 2 + core, g),
        )

    def send_c(i, _):
        g = tp_peer(i)
        c_copy(c, g, c, t).start()
        c_copy(1 - c, g, c, t).start()
        return 0

    c_copy(1 - c, t, c, t).start()
    lax.fori_loop(0, 15, send_c, 0)
    crecv[c, pl.ds(pl.multiple_of(t * 8, 8), 8), :] = csend[pl.ds(pl.multiple_of(t * 8, 8), 8), :]

    for way in range(2):
        first(way, 0).wait_recv()
        second(way).start()
        pair_near(way, 0).start()

    def wait_c(i, _):
        g = tp_peer(i)
        c_copy(c, g, c, g).wait_recv()
        c_copy(1 - c, g, 1 - c, g).wait_recv()
        return 0

    for j in range(4):
        w_local(j).wait()
        w_remote(j).wait_recv()
    c_copy(1 - c, t, 1 - c, t).wait_recv()
    lax.fori_loop(0, 15, wait_c, 0)

    flat = jnp.concatenate(
        [
            jnp.concatenate([crecv[core, pl.ds(r, 16, stride=8), :] for r in range(REQ)], axis=0)
            for core in range(2)
        ],
        axis=1,
    ).astype(jnp.bfloat16)

    def r1_copy(way, d, part):
        dst = lax.rem((x if way == 0 else z) + d, 4)
        src = (a_send if way == 0 else b_send).at[dst, pl.ds(part * 2, 2)]
        to = (a_recv if way == 0 else b_recv).at[d - 1, pl.ds(part * 2, 2)]
        return remote(
            src, to, r1s_sem.at[way, d - 1, part], r1r_sem.at[way, d - 1, part],
            (s, x_at(d) if way == 0 else z_at(d)),
        )

    def project(j, _):
        for i in range(4):
            piece = jnp.dot(flat, w_v[j, :, i * 512:(i + 1) * 512], preferred_element_type=jnp.float32)
            piece = piece.astype(jnp.bfloat16)
            a_send[i, j] = piece[:32]
            for k in range(4):
                b_send[k, j, :, i * 128:(i + 1) * 128] = piece[32:, k * 128:(k + 1) * 128]
        return 0

    for part in range(2):
        lax.fori_loop(part * 2, part * 2 + 2, project, 0)
        for d in (2, 1, 3):
            for way in range(2):
                r1_copy(way, d, part).start()

    for way in range(2):
        first(way, 1).wait_recv()
        pair_near(way, 1).start()

    def r2_copy(way, d, part):
        dst = lax.rem((z if way == 0 else x) + d, 4)
        src = (a2_send if way == 0 else b2_send).at[dst, pl.ds(part * 2, 2)]
        to = (a2_recv if way == 0 else b2_recv).at[d - 1, pl.ds(part * 2, 2)]
        return remote(
            src, to, r2s_sem.at[way, d - 1, part], r2r_sem.at[way, d - 1, part],
            (s, z_at(d) if way == 0 else x_at(d)),
        )

    for part in range(2):
        for way in range(2):
            for d in (1, 3, 2):
                r1_copy(way, d, part).wait_recv()
            send, recv, nxt = ((a_send, a_recv, a2_send), (b_send, b_recv, b2_send))[way]
            mine = x if way == 0 else z

            def add(j, _):
                out = send[mine, j].astype(jnp.float32)
                for d in range(3):
                    out = out + recv[d, j].astype(jnp.float32)
                out = out.astype(jnp.bfloat16)
                for k in range(4):
                    nxt[k, j] = out[:, k * 128:(k + 1) * 128]
                return 0

            lax.fori_loop(part * 2, part * 2 + 2, add, 0)
            for d in (2, 1, 3):
                r2_copy(way, d, part).start()

    h_copy.wait()
    g_copy.wait()
    for part in range(2):
        for way in range(2):
            for d in (1, 3, 2):
                r2_copy(way, d, part).wait_recv()
            send, recv = ((a2_send, a2_recv), (b2_send, b2_recv))[way]
            mine = z if way == 0 else x
            for j in range(part * 2, part * 2 + 2):
                out = send[mine, j].astype(jnp.float32)
                for d in range(3):
                    out = out + recv[d, j].astype(jnp.float32)
                y_send[j, way * 32:(way + 1) * 32, :] = out.astype(jnp.bfloat16)

    def y_copy(d):
        dst = lax.rem(y + d, 4)
        return remote(y_send.at[dst], y_recv.at[d - 1], ys_sem.at[d - 1], yr_sem.at[d - 1], (y_at(d), t))

    for d in (2, 1, 3):
        y_copy(d).start()

    for way in range(2):
        second(way).wait_recv()
        pair_far(way).start()

    rows_v[...] = hid_v[...].astype(jnp.float32)
    stream = jnp.concatenate([rows_v[pl.ds(r, 16, stride=REQ), :] for r in range(REQ)], axis=0)
    stream = stream + y_send[y].astype(jnp.float32)
    for d in (1, 3, 2):
        y_copy(d).wait_recv()
    for d in range(3):
        stream = stream + y_recv[d].astype(jnp.float32)

    squares = stream * stream
    squares = jnp.sum(jnp.concatenate([squares, squares], axis=0).T, axis=0, keepdims=True)
    n_send[...] = jnp.broadcast_to(squares, (8, 128))

    def n_copy(k, slot):
        return remote(n_send, n_recv.at[slot], ns_sem.at[k], nr_sem.at[slot], (k, t))

    def m_copy(k, slot):
        return remote(m_send, m_recv.at[slot], ms_sem.at[k], mr_sem.at[slot], (s, k))

    def send_n(i, _):
        n_copy(seq_peer(i), s).start()
        return 0

    def wait_n(i, so_far):
        k = seq_peer(i)
        n_copy(k, k).wait_recv()
        return so_far + n_recv[k]

    lax.fori_loop(0, 7, send_n, 0)
    for r in range(REQ):
        rows_v[pl.ds(r, 16, stride=REQ), :] = stream[r * 16:(r + 1) * 16]
    res_ref[...] = rows_v[...].astype(jnp.bfloat16)
    m_send[...] = lax.fori_loop(0, 7, wait_n, n_send[...])

    def send_m(i, _):
        m_copy(tp_peer(i), t).start()
        return 0

    def wait_m(i, so_far):
        k = tp_peer(i)
        m_copy(k, k).wait_recv()
        return so_far + m_recv[k]

    lax.fori_loop(0, 15, send_m, 0)
    squares = lax.fori_loop(0, 15, wait_m, m_send[...])
    scale = lax.rsqrt(squares[:1] / D + 1e-05)
    scale = jnp.broadcast_to(scale, (128, 128)).T[:64]
    normed = stream * scale * gain_v[...]
    for r in range(REQ):
        rows_v[pl.ds(r, 16, stride=REQ), :] = normed[r * 16:(r + 1) * 16]
    norm_ref[...] = rows_v[...].astype(jnp.bfloat16)

    for half in range(2):
        own[half].wait()
        pair_own(half).wait()
        for way in range(2):
            first(way, half).wait_send()
            pair_near(way, half).wait()
    for way in range(2):
        second(way).wait_send()
        pair_far(way).wait()
    for j in range(4):
        w_remote(j).wait_send()

    def drain_seq(i, _):
        k = seq_peer(i)
        l_copy(k, s).wait_send()
        o_copy(k, s).wait_send()
        n_copy(k, s).wait_send()
        return 0

    def drain_tp(i, _):
        k = tp_peer(i)
        c_copy(c, k, c, t).wait_send()
        c_copy(1 - c, k, c, t).wait_send()
        m_copy(k, t).wait_send()
        return 0

    lax.fori_loop(0, 7, drain_seq, 0)
    lax.fori_loop(0, 15, drain_tp, 0)
    c_copy(1 - c, t, c, t).wait_send()
    for way in range(2):
        for d in range(1, 4):
            for part in range(2):
                r1_copy(way, d, part).wait_send()
                r2_copy(way, d, part).wait_send()
    for d in range(1, 4):
        y_copy(d).wait_send()


def step(queries, cache_kv, new_kv, ctx_len, new_len, wo, hidden_in, norm_gain):
    bf, f32 = jnp.bfloat16, jnp.float32
    dma = pltpu.SemaphoreType.DMA
    anywhere = pl.BlockSpec(memory_space=pl.ANY)
    vmem = pl.BlockSpec(memory_space=pltpu.VMEM)
    smem = pl.BlockSpec(memory_space=pltpu.SMEM)
    V = pltpu.VMEM
    return pl.pallas_call(
        kernel,
        out_shape=(
            jax.ShapeDtypeStruct((64, 128), bf),
            jax.ShapeDtypeStruct((64, 128), bf),
            jax.ShapeDtypeStruct((REQ, KVH, WIDTH, 256), bf),
        ),
        in_specs=[smem, smem] + [anywhere] * 6,
        out_specs=(vmem, vmem, anywhere),
        scratch_shapes=[
            V((REQ, KVH, GROUP, HD), bf),
            V((REQ, KVH, KEYS, 256), bf),
            V((4, 256, 2048), bf),
            V((64, 128), bf),
            V((1, 128), f32),
            V((8, 64, HD), bf), V((8, 64, HD), bf),
            V((GROUP, 128), f32), V((8, GROUP, 128), f32),
            V((128, HD), f32), V((2, 128, HD), f32),
            V((4, 4, 32, 512), bf), V((4, 4, 32, 512), bf),
            V((3, 4, 32, 512), bf), V((3, 4, 32, 512), bf),
            V((4, 4, 32, 128), bf), V((4, 4, 32, 128), bf),
            V((3, 4, 32, 128), bf), V((3, 4, 32, 128), bf),
            V((4, 64, 128), bf), V((3, 64, 128), bf),
            V((8, 128), f32), V((8, 8, 128), f32),
            V((8, 128), f32), V((16, 8, 128), f32),
            V((64, 128), f32),
            dma((3,)), dma((REQ, 2)), dma((4,)), dma((4,)), dma((4,)),
            dma((8,)), dma((8,)), dma((8,)), dma((8,)), dma((2, 16)), dma((2, 16)),
            dma((2, 3, 2)), dma((2, 3, 2)), dma((2, 3, 2)), dma((2, 3, 2)), dma((3,)), dma((3,)),
            dma((8,)), dma((8,)), dma((16,)), dma((16,)),
            dma((2, 3)), dma((2, 3)), dma((8,)), dma((8,)), dma((2,)),
        ],
        compiler_params=pltpu.CompilerParams(
            collective_id=0, has_side_effects=True, vmem_limit_bytes=40 * 1024 * 1024
        ),
        cost_estimate=pl.CostEstimate(flops=600_000_000, bytes_accessed=14_000_000, transcendentals=1_000_000),
    )(ctx_len, new_len, queries, cache_kv, new_kv, wo, hidden_in, norm_gain.reshape(1, 128))


def per_device(queries, cache_kv, new_kv, ctx_len, new_len, owner, wo, hidden_in, norm_gain):
    seq_index = lax.axis_index("seq")
    tp_index = lax.axis_index("tp")
    residual_out, normed, delivered = step(
        queries, cache_kv, new_kv, ctx_len, new_len, wo, hidden_in, norm_gain
    )
    my_new = lax.dynamic_slice_in_dim(new_len, tp_index * REQ, REQ)
    my_owner = lax.dynamic_slice_in_dim(owner, tp_index * REQ, REQ)
    slots = jnp.arange(WIDTH, dtype=jnp.int32)
    kept = (my_owner == seq_index)[:, None] & (slots[None, :] < my_new[:, None])
    appended = jnp.where(kept[:, None, :, None], delivered, jnp.zeros((), jnp.bfloat16))
    return (residual_out, normed, appended)


def solution(mesh):
    in_specs = (
        P("tp", None, None, None),
        P("tp", None, "seq", None),
        P("tp", None, "seq", None),
        P(),
        P(),
        P(),
        P(("seq", "tp"), None),
        P(None, ("seq", "tp")),
        P(("seq", "tp")),
    )
    out_specs = (P(None, ("seq", "tp")), P(None, ("seq", "tp")), P("tp", None, "seq", None))
    return jax.shard_map(
        per_device, mesh=mesh, in_specs=in_specs, out_specs=out_specs, check_vma=False
    )
```

time: 815 us -> 73.1 us (0.09)
  waiting for transfers between devices: 644 us -> 0 us
  blocking collectives: 124 us -> 0 us
  Pallas kernels: 0 us -> 57.9 us
  other arithmetic: 17.9 us -> 3.21 us
  between operations: 13.9 us -> 0.65 us
  matrix products: 12.8 us -> 0 us
  local copies, waits for them, and re-layouts: 2.09 us -> 10.9 us
    reduce_scatter x1 -> x0, waiting for transfers between devices: 605 us -> none  [per_device(): lax.psum_scatter(lax.dot_general(wo, flat, (((0,), (1,)), ((), ())), pref...]
    psum x1 -> x0, blocking collectives: 93.5 us -> none  [per_device(): squares = lax.psum(jnp.sum(stream * stream, axis=1), ('seq', 'tp'))]
    pallas_call x0 -> x1, Pallas kernels: none -> 57.9 us  [step(): pl.pallas_call(kernel, out_shape=(jax.ShapeDtypeStruct((64, 128), bf), ja...]
    all_gather x2 -> x0, waiting for transfers between devices: 37.7 us -> none  [the longest x1 32.9 us: per_device(): delivered = lax.all_gather(new_kv, 'seq', axis=2, tiled=True)]
    all_gather x2 -> x0, blocking collectives: 17.7 us -> none  [joined(): lax.all_gather(part.astype(kind), axis)]
    all_to_all x1 -> x0, blocking collectives: 12.9 us -> none  [per_device(): lax.all_to_all(context, 'tp', split_axis=1, concat_axis=0, tiled=True)]
    dot_general x5 -> x0, matrix products: 12.8 us -> none  [the longest x1 4.86 us: per_device(): lax.dot_general(wo, flat, (((0,), (1,)), ((), ())), preferred_element_typ...]
    unnamed x8 -> x18, local copies, waits for them, and re-layouts: 0.03 us -> 10.2 us
  transfers between devices with their start and end apart: 3 -> 0, of which waited for: 3 -> 0; matrix products, arithmetic and copies ran while one was open for 1% -> 0% of each run, Pallas kernels for 0% -> 0%
where the time goes in v1:
time: 73.1 us; the launch traced here: 72.7 us
  Pallas kernels  57.9 us (79%)
  local copies, waits for them, and re-layouts  10.9 us (15%)
  other arithmetic  3.21 us (4%)
    pallas_call x1, Pallas kernels, step(): pl.pallas_call(kernel, out_shape=(jax.ShapeDtypeStruct((64, 128), bf), ja...  57.9 us
    unnamed x18, local copies, waits for them, and re-layouts  10.2 us
    select_n x1, other arithmetic, per_device(): jnp.where(kept[:, None, :, None], delivered, jnp.zeros((), jnp.bfloat16))  2.39 us

profile of v1, /device:TPU:1, one launch (start us, length us, event | category | flops | bytes accessed | tf_op | source)
XLA Modules:
  0.0 72.7 jit_solution(12282233395990518366)
XLA Ops:
  0.6 0.7 %dynamic-slice_compare_fusion = pred[4]{0:T(512)(128)(4,1)S(1)} fusion(s32[64]{0:T(128)} %param.14, s32[]{:T(128)S(6)} %select_n.8, s32[]{:T(128)S(6)} %axis_index.25), kind=kLoop, calls=%fused_computation.3 | loop fusion | flops 4 | bytes 28 | tf_op jit(solution)/shard_map/eq | solution.py:485
  1.4 0.7 %dynamic_slice.7 = s32[4]{0:T(128)S(1)} dynamic-slice(s32[64]{0:T(128)} %new_ref.1, s32[]{:T(128)S(6)} %select_n.8), dynamic_slice_sizes={4} | dynamic-slice | bytes 36 | tf_op jit(solution)/shard_map/dynamic_slice | solution.py:482
  2.1 0.1 fusion
  2.2 0.0 copy-start
  2.2 2.2 %copy-done = bf16[4,8,256,256]{3,2,1,0:T(8,128)(2,1)S(1)} copy-done((bf16[4,8,256,256]{3,2,1,0:T(8,128)(2,1)S(1)}, bf16[4,8,256,256]{3,2,1,0:T(8,128)(2,1)}, u32[]{:S(2)}) %copy-start) | copy-done | bytes 4194328
  4.4 0.0 copy-start.1
  4.4 2.2 %copy-done.1 = bf16[128,16384]{1,0:T(8,128)(2,1)S(1)} copy-done((bf16[128,16384]{1,0:T(8,128)(2,1)S(1)}, bf16[128,16384]{1,0:T(8,128)(2,1)}, u32[]{:S(2)}) %copy-start.1) | copy-done | bytes 4194328
  6.6 0.0 copy-start.2
  6.6 1.0 %copy-done.2 = bf16[4,8,32,256]{3,2,1,0:T(8,128)(2,1)S(1)} copy-done((bf16[4,8,32,256]{3,2,1,0:T(8,128)(2,1)S(1)}, bf16[4,8,32,256]{3,2,1,0:T(8,128)(2,1)}, u32[]{:S(2)}) %copy-start.2) | copy-done | bytes 524312
  7.6 0.0 copy-start.3
  7.6 0.9 %copy-done.3 = bf16[4,8,16,128]{3,2,1,0:T(8,128)(2,1)S(1)} copy-done((bf16[4,8,16,128]{3,2,1,0:T(8,128)(2,1)S(1)}, bf16[4,8,16,128]{3,2,1,0:T(8,128)(2,1)}, u32[]{:S(2)}) %copy-start.3) | copy-done | bytes 131096
  8.5 0.0 copy-start.4
  8.5 0.7 copy-done.4
  9.2 0.0 copy-start.5
  9.2 0.7 copy-done.5
  9.9 0.0 copy-start.6
  9.9 0.7 copy-done.6
  10.5 0.0 copy-start.7
  10.5 0.7 copy-done.7
  11.2 57.9 %shard_map.112 = (bf16[64,128]{1,0:T(8,128)(2,1)S(1)}, bf16[64,128]{1,0:T(8,128)(2,1)S(1)}, bf16[4,8,256,256]{3,2,1,0:T(8,128)(2,1)S(1)}) custom-call(s32[64]{0:T(128)S(1)} %copy-done.5, s32[64]{0:T(128)S(1)} %copy-done.6, bf16[4,8,16,128]{3,2,1,0:T(8,128)(2,1)S(1)} %copy-done.3, bf16[4,8,256,256]{3,2,1,0:T(8,128)(2,1)S(1)} %copy-done, ...), custom_call_target="tpu_custom_call" | custom-call | flops 600000000 | bytes 14000000 | tf_op jit(solution)/shard_map/pallas_call | solution.py:437
  69.1 2.4 %broadcast_select_fusion = bf16[4,8,256,256]{3,2,1,0:T(8,128)(2,1)} fusion(bf16[4,8,256,256]{3,2,1,0:T(8,128)(2,1)S(1)} %get-tuple-element.8, pred[4,256]{1,0:T(4,128)(4,1)S(1)} %fusion), kind=kLoop, calls=%fused_computation | loop fusion | flops 2097152 | bytes 8389632 | tf_op jit(solution)/shard_map/jit(_where)/select_n | solution.py:486
  71.5 0.6 copy.14
  72.1 0.6 copy.15
Async XLA Ops:
  2.2 2.2 %copy-start = (bf16[4,8,256,256]{3,2,1,0:T(8,128)(2,1)S(1)}, bf16[4,8,256,256]{3,2,1,0:T(8,128)(2,1)}, u32[]{:S(2)}) copy-start(bf16[4,8,256,256]{3,2,1,0:T(8,128)(2,1)} %cache_hbm.1) | copy-start | bytes 12582916
  4.4 2.2 %copy-start.1 = (bf16[128,16384]{1,0:T(8,128)(2,1)S(1)}, bf16[128,16384]{1,0:T(8,128)(2,1)}, u32[]{:S(2)}) copy-start(bf16[128,16384]{1,0:T(8,128)(2,1)} %wo_hbm.1) | copy-start | bytes 12582916
  6.6 1.0 %copy-start.2 = (bf16[4,8,32,256]{3,2,1,0:T(8,128)(2,1)S(1)}, bf16[4,8,32,256]{3,2,1,0:T(8,128)(2,1)}, u32[]{:S(2)}) copy-start(bf16[4,8,32,256]{3,2,1,0:T(8,128)(2,1)} %newkv_hbm.1) | copy-start | bytes 1572868
  7.6 0.9 %copy-start.3 = (bf16[4,8,16,128]{3,2,1,0:T(8,128)(2,1)S(1)}, bf16[4,8,16,128]{3,2,1,0:T(8,128)(2,1)}, u32[]{:S(2)}) copy-start(bf16[4,8,16,128]{3,2,1,0:T(8,128)(2,1)} %q_hbm.1) | copy-start | bytes 393220
  8.5 0.7 copy-start.4
  9.2 0.7 copy-start.5
  9.9 0.7 copy-start.6
  10.5 0.7 copy-start.7

commit v2 on v1

--- a/solution.py
+++ b/solution.py
@@ -467,24 +467,88 @@
             dma((2, 3)), dma((2, 3)), dma((8,)), dma((8,)), dma((2,)),
         ],
         compiler_params=pltpu.CompilerParams(
-            collective_id=0, has_side_effects=True, vmem_limit_bytes=40 * 1024 * 1024
+            collective_id=0, has_side_effects=True, vmem_limit_bytes=62 * 1024 * 1024
         ),
         cost_estimate=pl.CostEstimate(flops=600_000_000, bytes_accessed=14_000_000, transcendentals=1_000_000),
     )(ctx_len, new_len, queries, cache_kv, new_kv, wo, hidden_in, norm_gain.reshape(1, 128))
 
 
+def store_kernel(owner_ref, new_ref, res_in, norm_in, deliv_hbm, res_ref, norm_ref, app_hbm, zeros, held, out_sem, in_sem):
+    s = lax.axis_index("seq")
+    t = lax.axis_index("tp")
+
+    def blank(r, i):
+        return pltpu.make_async_copy(zeros, app_hbm.at[r, pl.ds(i * 2, 2)], out_sem.at[r, i])
+
+    def fetch(r):
+        return pltpu.make_async_copy(deliv_hbm.at[r], held.at[r], in_sem.at[r])
+
+    def put(r):
+        return pltpu.make_async_copy(held.at[r], app_hbm.at[r], in_sem.at[r])
+
+    zeros[...] = jnp.zeros_like(zeros)
+    for r in range(REQ):
+        mine = owner_ref[t * REQ + r] == s
+
+        @pl.when(mine)
+        def _():
+            fetch(r).start()
+
+        @pl.when(jnp.logical_not(mine))
+        def _():
+            for i in range(4):
+                blank(r, i).start()
+
+    res_ref[...] = res_in[...]
+    norm_ref[...] = norm_in[...]
+    slot = lax.broadcasted_iota(jnp.int32, (WIDTH, 256), 0)
+    for r in range(REQ):
+        @pl.when(owner_ref[t * REQ + r] == s)
+        def _():
+            fetch(r).wait()
+            live = slot < new_ref[t * REQ + r]
+            for h in range(KVH):
+                held[r, h] = jnp.where(live, held[r, h], jnp.zeros((), jnp.bfloat16))
+            put(r).start()
+
+    for r in range(REQ):
+        mine = owner_ref[t * REQ + r] == s
+
+        @pl.when(mine)
+        def _():
+            put(r).wait()
+
+        @pl.when(jnp.logical_not(mine))
+        def _():
+            for i in range(4):
+                blank(r, i).wait()
+
+
+def store(owner, new_len, residual_out, normed, delivered):
+    anywhere = pl.BlockSpec(memory_space=pl.ANY)
+    vmem = pl.BlockSpec(memory_space=pltpu.VMEM)
+    smem = pl.BlockSpec(memory_space=pltpu.SMEM)
+    return pl.pallas_call(
+        store_kernel,
+        out_shape=tuple(jax.ShapeDtypeStruct(v.shape, v.dtype) for v in (residual_out, normed, delivered)),
+        in_specs=[smem, smem, vmem, vmem, anywhere],
+        out_specs=(vmem, vmem, anywhere),
+        scratch_shapes=[
+            pltpu.VMEM((2, WIDTH, 256), jnp.bfloat16),
+            pltpu.VMEM((REQ, KVH, WIDTH, 256), jnp.bfloat16),
+            pltpu.SemaphoreType.DMA((REQ, 4)),
+            pltpu.SemaphoreType.DMA((REQ,)),
+        ],
+        compiler_params=pltpu.CompilerParams(vmem_limit_bytes=62 * 1024 * 1024),
+        cost_estimate=pl.CostEstimate(flops=0, bytes_accessed=6_000_000, transcendentals=0),
+    )(owner, new_len, residual_out, normed, delivered)
+
+
 def per_device(queries, cache_kv, new_kv, ctx_len, new_len, owner, wo, hidden_in, norm_gain):
-    seq_index = lax.axis_index("seq")
-    tp_index = lax.axis_index("tp")
     residual_out, normed, delivered = step(
         queries, cache_kv, new_kv, ctx_len, new_len, wo, hidden_in, norm_gain
     )
-    my_new = lax.dynamic_slice_in_dim(new_len, tp_index * REQ, REQ)
-    my_owner = lax.dynamic_slice_in_dim(owner, tp_index * REQ, REQ)
-    slots = jnp.arange(WIDTH, dtype=jnp.int32)
-    kept = (my_owner == seq_index)[:, None] & (slots[None, :] < my_new[:, None])
-    appended = jnp.where(kept[:, None, :, None], delivered, jnp.zeros((), jnp.bfloat16))
-    return (residual_out, normed, appended)
+    return store(owner, new_len, residual_out, normed, delivered)
 
 
 def solution(mesh):

time: 73.1 us -> 64.4 us (0.88)
  local copies, waits for them, and re-layouts: 10.9 us -> 0 us
  Pallas kernels: 57.9 us -> 63.6 us
  other arithmetic: 3.21 us -> 0 us
    unnamed x18 -> x0, local copies, waits for them, and re-layouts: 10.2 us -> none
    pallas_call x0 -> x1, Pallas kernels: none -> 4.63 us  [store(): pl.pallas_call(store_kernel, out_shape=tuple((jax.ShapeDtypeStruct(v.shap...]
    select_n x1 -> x0, other arithmetic: 2.39 us -> none  [per_device(): jnp.where(kept[:, None, :, None], delivered, jnp.zeros((), jnp.bfloat16))]
    pallas_call x1, Pallas kernels: 57.9 us -> 59 us  [step(): pl.pallas_call(kernel, out_shape=(jax.ShapeDtypeStruct((64, 128), bf), ja...]
    eq x1 -> x0, other arithmetic: 0.74 us -> none  [per_device(): kept = (my_owner == seq_index)[:, None] & (slots[None, :] < my_new[:, None])]
where the time goes in v2:
time: 64.4 us; the launch traced here: 64.2 us
  Pallas kernels  63.6 us (99%)
    pallas_call x1, Pallas kernels, step(): pl.pallas_call(kernel, out_shape=(jax.ShapeDtypeStruct((64, 128), bf), ja...  59 us
    pallas_call x1, Pallas kernels, store(): pl.pallas_call(store_kernel, out_shape=tuple((jax.ShapeDtypeStruct(v.shap...  4.63 us

profile of v2, /device:TPU:1, one launch (start us, length us, event | category | flops | bytes accessed | tf_op | source)
XLA Modules:
  0.0 64.2 jit_solution(5021116461519830732)
XLA Ops:
  0.6 59.0 %shard_map.112 = (bf16[64,128]{1,0:T(8,128)(2,1)}, bf16[64,128]{1,0:T(8,128)(2,1)}, bf16[4,8,256,256]{3,2,1,0:T(8,128)(2,1)}) custom-call(s32[64]{0:T(128)} %ctx_ref.1, s32[64]{0:T(128)} %new_ref.3, bf16[4,8,16,128]{3,2,1,0:T(8,128)(2,1)} %q_hbm.1, bf16[4,8,256,256]{3,2,1,0:T(8,128)(2,1)} %cache_hbm.1, bf16[4,8,32,256]{3,2,1,0:T(8,128)(2,1)} %newkv_hbm.1, ...), custom_call_target="tpu_custom_call" | custom-call | flops 600000000 | bytes 14000000 | tf_op jit(solution)/shard_map/pallas_call | solution.py:437
  59.6 4.6 %shard_map.113 = (bf16[64,128]{1,0:T(8,128)(2,1)}, bf16[64,128]{1,0:T(8,128)(2,1)}, bf16[4,8,256,256]{3,2,1,0:T(8,128)(2,1)}) custom-call(s32[64]{0:T(128)} %owner_ref.1, s32[64]{0:T(128)} %new_ref.3, bf16[64,128]{1,0:T(8,128)(2,1)} %get-tuple-element.6.res_in, bf16[64,128]{1,0:T(8,128)(2,1)} %get-tuple-element.7.norm_in, ...), custom_call_target="tpu_custom_call" | custom-call | bytes 6000000 | tf_op jit(solution)/shard_map/pallas_call | solution.py:531

commit v3 on v2

v3 whole, which is shorter than its diff:
```python
import functools

import jax
import jax.numpy as jnp
from jax import lax
from jax.experimental import pallas as pl
from jax.experimental.pallas import tpu as pltpu
from jax.sharding import PartitionSpec as P

D = 16384
HD = 128
KVH = 8
GROUP = 16
REQ = 4
WIDTH = 256
SHARE = 32
KEYS = WIDTH + SHARE
NEG = -1e30
MESH = pl.DeviceIdType.MESH


def remote(src, dst, send, recv, device):
    return pltpu.make_async_remote_copy(
        src_ref=src, dst_ref=dst, send_sem=send, recv_sem=recv, device_id=device, device_id_type=MESH
    )


def kernel(
    ctx_hbm, new_hbm, q_hbm, cache_hbm, newkv_hbm, wo_hbm, hidden_hbm, gain_hbm,
    res_hbm, norm_hbm, deliv_hbm,
    ctx_s, new_s, q_v, kv, fresh, w_v, hid_v, gain_v,
    osend, orecv, csend, crecv,
    a_send, b_send, a_recv, b_recv, a2_send, b2_send, a2_recv, b2_recv,
    n_send, n_recv, rows_v, res_v, norm_v,
    loc_sem, out_sem, kv_sem, wl_sem, ws_sem, wr_sem,
    os_sem, or_sem, cs_sem, cr_sem,
    r1s_sem, r1r_sem, r2s_sem, r2r_sem, ns_sem, nr_sem,
    gs_sem, gr_sem, ps_sem, pr_sem, gl_sem,
):
    s = lax.axis_index("seq")
    t = lax.axis_index("tp")
    y, c = s // 2, s % 2
    x, z = t // 4, t % 4
    me = s * 16 + t
    sp = y * 2 + (1 - c)

    def seq_peer(i):
        return lax.rem(s + 1 + i, 8)

    def tp_peer(i):
        return lax.rem(t + 1 + i, 16)

    def any_peer(i):
        k = lax.rem(me + 1 + i, 128)
        return k // 16, lax.rem(k, 16)

    def y_at(d):
        return lax.rem(y + d, 4) * 2 + c

    def x_at(d):
        return lax.rem(x + d, 4) * 4 + z

    def z_at(d):
        return x * 4 + lax.rem(z + d, 4)

    drains = []

    loads = [
        pltpu.make_async_copy(src, dst, loc_sem.at[i])
        for i, (src, dst) in enumerate(
            [(ctx_hbm, ctx_s), (new_hbm, new_s), (q_hbm, q_v), (hidden_hbm, hid_v), (gain_hbm, gain_v)]
        )
    ]

    def kv_copies(r):
        return (
            pltpu.make_async_copy(cache_hbm.at[r], kv.at[r, :, pl.ds(0, WIDTH), :], kv_sem.at[r, 0]),
            pltpu.make_async_copy(newkv_hbm.at[r], kv.at[r, :, pl.ds(WIDTH, SHARE), :], kv_sem.at[r, 1]),
        )

    for load in loads[:3]:
        load.start()
    for r in range(REQ):
        for copy in kv_copies(r):
            copy.start()
    for load in loads[3:]:
        load.start()

    barrier = pltpu.get_barrier_semaphore()

    def greet(i, _):
        pl.semaphore_signal(barrier, inc=1, device_id=any_peer(i), device_id_type=MESH)
        return 0

    lax.fori_loop(0, 127, greet, 0)

    def w_local(j):
        return pltpu.make_async_copy(
            wo_hbm.at[:, pl.ds(pl.multiple_of(j * 4096 + c * 2048, 2048), 2048)],
            w_v.at[j, pl.ds(pl.multiple_of(c * 128, 128), 128), :],
            wl_sem.at[j],
        )

    def w_remote(j):
        return remote(
            wo_hbm.at[:, pl.ds(pl.multiple_of(j * 4096 + (1 - c) * 2048, 2048), 2048)],
            w_v.at[j, pl.ds(pl.multiple_of(c * 128, 128), 128), :],
            ws_sem.at[j], wr_sem.at[j], (sp, t),
        )

    for j in range(4):
        w_local(j).start()

    def block(half, who):
        return deliv_hbm.at[pl.ds(half * 2, 2), :, pl.ds(pl.multiple_of(who * SHARE, SHARE), SHARE), :]

    own = [
        pltpu.make_async_copy(fresh.at[pl.ds(half * 2, 2)], block(half, s), gl_sem.at[half])
        for half in range(2)
    ]

    def ring(way, slot, src, dst):
        return remote(src, dst, gs_sem.at[way, slot], gr_sem.at[way, slot], (y_at(1 if way == 0 else 3), t))

    def first(way, order):
        half = order if way == 0 else 1 - order
        return ring(way, order, fresh.at[pl.ds(half * 2, 2)], block(half, s))

    def second(way):
        who = y_at(3) if way == 0 else y_at(1)
        return ring(way, 2, block(way, who), block(way, who))

    def pair(slot, src, half, who):
        return remote(src, block(half, who), ps_sem.at[slot], pr_sem.at[slot], (sp, t))

    def pair_own(half):
        return pair(half, fresh.at[pl.ds(half * 2, 2)], half, s)

    def pair_near(way, order):
        half = order if way == 0 else 1 - order
        who = y_at(3) if way == 0 else y_at(1)
        return pair(2 + way * 2 + order, block(half, who), half, who)

    def pair_far(way):
        return pair(6 + way, block(way, y_at(2)), way, y_at(2))

    col = lax.broadcasted_iota(jnp.int32, (KVH * GROUP, KEYS), 1)
    lane = lax.broadcasted_iota(jnp.int32, (KVH * GROUP, 128), 1)

    def attend(r, stats):
        for copy in kv_copies(r):
            copy.wait()
        live_ctx = jnp.minimum(ctx_s[t * REQ + r] - s * WIDTH, WIDTH)
        live_new = new_s[t * REQ + r] - s * SHARE + WIDTH
        mask = (col < live_ctx) | ((col >= WIDTH) & (col < live_new))
        scores = jnp.concatenate(
            [
                lax.dot_general(
                    q_v[r, h], kv[r, h, :, :HD], (((1,), (1,)), ((), ())), preferred_element_type=jnp.float32
                )
                for h in range(KVH)
            ],
            axis=0,
        ) * HD ** (-0.5)
        scores = jnp.where(mask, scores, NEG)
        top = jnp.max(scores, axis=1, keepdims=True)
        weights = jnp.where(mask, jnp.exp(scores - top), 0.0)
        total = jnp.maximum(jnp.sum(weights, axis=1, keepdims=True), 1e-30)
        weights = weights.astype(jnp.bfloat16)
        inverse = 1.0 / total
        for h in range(KVH):
            rows = slice(h * GROUP, (h + 1) * GROUP)
            out = jnp.dot(weights[rows], kv[r, h, :, HD:], preferred_element_type=jnp.float32)
            osend[h, r * GROUP:(r + 1) * GROUP, :] = (out * inverse[rows]).astype(jnp.bfloat16)
        return jnp.where(lane == r, top + jnp.log(total), stats)

    def rows_of(part):
        return pl.ds(0, 32) if part == 0 else pl.ds(32, 48)

    def o_copy(k, part):
        return remote(
            osend.at[k, rows_of(part)], orecv.at[s, rows_of(part)], os_sem.at[part], or_sem.at[part], (k, t)
        )

    def o_own(part):
        return pltpu.make_async_copy(
            osend.at[s, rows_of(part)], orecv.at[s, rows_of(part)], or_sem.at[part]
        )

    def send_o(part):
        o_own(part).start()

        def one(i, _):
            o_copy(seq_peer(i), part).start()
            return 0

        lax.fori_loop(0, 7, one, 0)

    def wait_o(part):
        everything = orecv.at[:, rows_of(part)]
        pltpu.make_async_copy(everything, everything, or_sem.at[part]).wait()

    def drain_o():
        for part in range(2):
            sent = osend.at[pl.ds(0, 7), rows_of(part)]
            pltpu.make_async_copy(sent, sent, os_sem.at[part]).wait()

    for load in loads[:3]:
        load.wait()
    stats = jnp.zeros((KVH * GROUP, 128), jnp.float32)
    stats = attend(0, stats)
    stats = attend(1, stats)
    pl.semaphore_wait(barrier, 127)
    drains.append(drain_o)
    send_o(0)
    for j in range(4):
        w_remote(j).start()
    stats = attend(2, stats)
    stats = attend(3, stats)
    high = stats.astype(jnp.bfloat16).astype(jnp.float32)
    middle = (stats - high).astype(jnp.bfloat16).astype(jnp.float32)
    low = stats - high - middle
    pieces = (high + pltpu.roll(middle, 4, 1) + pltpu.roll(low, 8, 1)).astype(jnp.bfloat16)
    for h in range(KVH):
        osend[h, 64:80, :] = pieces[h * GROUP:(h + 1) * GROUP]
    send_o(1)

    slot = lax.broadcasted_iota(jnp.int32, (SHARE, 256), 0)
    for r in range(REQ):
        live = slot < new_s[t * REQ + r] - s * SHARE
        for h in range(KVH):
            fresh[r, h] = jnp.where(live, kv[r, h, WIDTH:, :], jnp.zeros((), jnp.bfloat16))

    def drain_gather():
        for half in range(2):
            own[half].wait()
            pair_own(half).wait()
            for way in range(2):
                first(way, half).wait_send()
                pair_near(way, half).wait()
        for way in range(2):
            second(way).wait_send()
            pair_far(way).wait()

    def drain_w():
        for j in range(4):
            w_remote(j).wait_send()

    drains.append(drain_gather)
    drains.append(drain_w)

    wait_o(0)
    wait_o(1)
    for order in range(2):
        for way in range(2):
            first(way, order).start()
    for half in range(2):
        own[half].start()
        pair_own(half).start()

    tops = []
    for k in range(8):
        piece = orecv[k, 64:80, :].astype(jnp.float32)
        tops.append(piece + pltpu.roll(piece, 124, 1) + pltpu.roll(piece, 120, 1))
    top = functools.reduce(jnp.maximum, tops)
    exps = [jnp.exp(v - top) for v in tops]
    total = functools.reduce(jnp.add, exps)
    shares = [e / total for e in exps]
    for r in range(REQ):
        context = jnp.zeros((GROUP, HD), jnp.float32)
        for k in range(8):
            part = orecv[k, r * GROUP:(r + 1) * GROUP, :].astype(jnp.float32)
            context = context + part * shares[k][:, r:r + 1]
        csend[:, r, :] = context

    def c_copy(core, g):
        return remote(
            csend.at[g], crecv.at[c, t], cs_sem.at[0], cr_sem.at[0], (y * 2 + core, g)
        )

    def send_c(i, _):
        g = tp_peer(i)
        c_copy(c, g).start()
        c_copy(1 - c, g).start()
        return 0

    def drain_c():
        for sent in (csend, csend.at[pl.ds(0, 15)]):
            pltpu.make_async_copy(sent, sent, cs_sem.at[0]).wait()

    drains.append(drain_c)
    lax.fori_loop(0, 15, send_c, 0)
    c_copy(1 - c, t).start()
    pltpu.make_async_copy(csend.at[t], crecv.at[c, t], cr_sem.at[0]).start()
    for j in range(4):
        w_local(j).wait()
        w_remote(j).wait_recv()
    pltpu.make_async_copy(crecv, crecv, cr_sem.at[0]).wait()

    flat = jnp.concatenate(
        [
            jnp.concatenate([crecv[core, :, r, :] for r in range(REQ)], axis=0)
            for core in range(2)
        ],
        axis=1,
    ).astype(jnp.bfloat16)

    def r1_copy(way, d, part):
        dst = lax.rem((x if way == 0 else z) + d, 4)
        src = (a_send if way == 0 else b_send).at[dst, pl.ds(part * 2, 2)]
        to = (a_recv if way == 0 else b_recv).at[d - 1, pl.ds(part * 2, 2)]
        return remote(
            src, to, r1s_sem.at[way, d - 1, part], r1r_sem.at[way, d - 1, part],
            (s, x_at(d) if way == 0 else z_at(d)),
        )

    def project(j, _):
        for i in range(4):
            piece = jnp.dot(flat, w_v[j, :, i * 512:(i + 1) * 512], preferred_element_type=jnp.float32)
            piece = piece.astype(jnp.bfloat16)
            a_send[i, j] = piece[:32]
            for k in range(4):
                b_send[k, j, :, i * 128:(i + 1) * 128] = piece[32:, k * 128:(k + 1) * 128]
        return 0

    def drain_r1():
        for way in range(2):
            for d in range(1, 4):
                for part in range(2):
                    r1_copy(way, d, part).wait_send()

    drains.append(drain_r1)
    for part in range(2):
        lax.fori_loop(part * 2, part * 2 + 2, project, 0)
        for d in (2, 1, 3):
            for way in range(2):
                r1_copy(way, d, part).start()

    def r2_copy(way, j, k):
        there = z if way == 0 else x
        send, recv = ((a2_send, a2_recv), (b2_send, b2_recv))[way]
        return remote(
            send.at[j, k], recv.at[y, there], r2s_sem.at[way], r2r_sem.at[way],
            (j * 2 + c, x * 4 + k if way == 0 else k * 4 + z),
        )

    def drain_r2():
        for way in range(2):
            send = (a2_send, b2_send)[way]
            for sent in (send.at[pl.ds(0, 3)], send.at[0, pl.ds(0, 3)]):
                pltpu.make_async_copy(sent, sent, r2s_sem.at[way]).wait()

    drains.append(drain_r2)
    for part in range(2):
        for way in range(2):
            for d in (1, 3, 2):
                r1_copy(way, d, part).wait_recv()
            send, recv, nxt = ((a_send, a_recv, a2_send), (b_send, b_recv, b2_send))[way]
            last = ((a2_send, a2_recv), (b2_send, b2_recv))[way]
            mine = x if way == 0 else z
            there = z if way == 0 else x

            def add(j, _):
                out = send[mine, j].astype(jnp.float32)
                for d in range(3):
                    out = out + recv[d, j].astype(jnp.float32)
                out = out.astype(jnp.bfloat16)
                for k in range(4):
                    nxt[j, k] = out[:, k * 128:(k + 1) * 128]
                for k in range(4):
                    away = (j != y) | (k != there)

                    @pl.when(away)
                    def _():
                        r2_copy(way, j, k).start()

                    @pl.when(jnp.logical_not(away))
                    def _():
                        pltpu.make_async_copy(nxt.at[j, k], last[1].at[j, k], r2r_sem.at[way]).start()
                return 0

            lax.fori_loop(part * 2, part * 2 + 2, add, 0)
        if part == 0:
            for way in range(2):
                first(way, 0).wait_recv()
                second(way).start()
                pair_near(way, 0).start()

    for load in loads[3:]:
        load.wait()
    rows_v[...] = hid_v[...].astype(jnp.float32)
    stream = jnp.concatenate([rows_v[pl.ds(r, 16, stride=REQ), :] for r in range(REQ)], axis=0)
    for way in range(2):
        first(way, 1).wait_recv()
        pair_near(way, 1).start()
    sums = []
    for way in range(2):
        recv = (a2_recv, b2_recv)[way]
        pltpu.make_async_copy(recv, recv, r2r_sem.at[way]).wait()
        out = recv[0, 0].astype(jnp.float32)
        for i in range(1, 16):
            out = out + recv[i // 4, i % 4].astype(jnp.float32)
        sums.append(out)
    stream = stream + jnp.concatenate(sums, axis=0)

    squares = stream * stream
    n_send[...] = jnp.sum(jnp.concatenate([squares, squares], axis=0).T, axis=0, keepdims=True)

    def send_n(i, _):
        pltpu.make_async_remote_copy(
            src_ref=n_send, dst_ref=n_recv.at[me], send_sem=ns_sem.at[0], recv_sem=nr_sem.at[0],
            device_id=any_peer(i), device_id_type=MESH,
        ).start()
        return 0

    def drain_n():
        sent = n_recv.at[pl.ds(0, 127)]
        pltpu.make_async_copy(sent, sent, ns_sem.at[0]).wait()

    drains.append(drain_n)
    lax.fori_loop(0, 127, send_n, 0)
    pltpu.make_async_copy(n_send, n_recv.at[me], nr_sem.at[0]).start()
    for r in range(REQ):
        rows_v[pl.ds(r, 16, stride=REQ), :] = stream[r * 16:(r + 1) * 16]
    res_v[...] = rows_v[...].astype(jnp.bfloat16)
    res_out = pltpu.make_async_copy(res_v, res_hbm, out_sem.at[0])
    res_out.start()
    for way in range(2):
        second(way).wait_recv()
        pair_far(way).start()
    scaled = stream * gain_v[...]
    pltpu.make_async_copy(n_recv, n_recv, nr_sem.at[0]).wait()
    scale = lax.rsqrt(jnp.sum(n_recv[...], axis=0) / D + 1e-05)
    scale = jnp.broadcast_to(scale, (128, 128)).T[:64]
    normed = scaled * scale
    for r in range(REQ):
        rows_v[pl.ds(r, 16, stride=REQ), :] = normed[r * 16:(r + 1) * 16]
    norm_v[...] = rows_v[...].astype(jnp.bfloat16)
    norm_out = pltpu.make_async_copy(norm_v, norm_hbm, out_sem.at[1])
    norm_out.start()
    res_out.wait()
    norm_out.wait()
    for drain in drains:
        drain()


def step(queries, cache_kv, new_kv, ctx_len, new_len, wo, hidden_in, norm_gain):
    bf, f32 = jnp.bfloat16, jnp.float32
    dma = pltpu.SemaphoreType.DMA
    anywhere = pl.BlockSpec(memory_space=pl.ANY)
    V = pltpu.VMEM
    return pl.pallas_call(
        kernel,
        out_shape=(
            jax.ShapeDtypeStruct((64, 128), bf),
            jax.ShapeDtypeStruct((64, 128), bf),
            jax.ShapeDtypeStruct((REQ, KVH, WIDTH, 256), bf),
        ),
        in_specs=[anywhere] * 8,
        out_specs=(anywhere, anywhere, anywhere),
        scratch_shapes=[
            pltpu.SMEM((64,), jnp.int32), pltpu.SMEM((64,), jnp.int32),
            V((REQ, KVH, GROUP, HD), bf),
            V((REQ, KVH, KEYS, 256), bf),
            V((REQ, KVH, SHARE, 256), bf),
            V((4, 256, 2048), bf),
            V((64, 128), bf),
            V((1, 128), f32),
            V((8, 80, HD), bf), V((8, 80, HD), bf),
            V((16, REQ, HD), f32), V((2, 16, REQ, HD), f32),
            V((4, 4, 32, 512), bf), V((4, 4, 32, 512), bf),
            V((3, 4, 32, 512), bf), V((3, 4, 32, 512), bf),
            V((4, 4, 32, 128), bf), V((4, 4, 32, 128), bf),
            V((4, 4, 32, 128), bf), V((4, 4, 32, 128), bf),
            V((1, 128), f32), V((128, 1, 128), f32),
            V((64, 128), f32), V((64, 128), bf), V((64, 128), bf),
            dma((5,)), dma((2,)), dma((REQ, 2)), dma((4,)), dma((4,)), dma((4,)),
            dma((2,)), dma((2,)), dma((1,)), dma((1,)),
            dma((2, 3, 2)), dma((2, 3, 2)), dma((2,)), dma((2,)), dma((1,)), dma((1,)),
            dma((2, 3)), dma((2, 3)), dma((8,)), dma((8,)), dma((2,)),
        ],
        compiler_params=pltpu.CompilerParams(
            collective_id=0, has_side_effects=True, vmem_limit_bytes=62 * 1024 * 1024
        ),
        cost_estimate=pl.CostEstimate(flops=600_000_000, bytes_accessed=14_000_000, transcendentals=1_000_000),
    )(ctx_len, new_len, queries, cache_kv, new_kv, wo, hidden_in, norm_gain.reshape(1, 128))


def store_kernel(owner_ref, res_in, norm_in, deliv_hbm, res_hbm, norm_hbm, app_hbm, zeros, out_sem, sem):
    s = lax.axis_index("seq")
    t = lax.axis_index("tp")
    small = (
        pltpu.make_async_copy(res_in, res_hbm, sem.at[0]),
        pltpu.make_async_copy(norm_in, norm_hbm, sem.at[1]),
    )
    for copy in small:
        copy.start()

    def blank(r, i):
        return pltpu.make_async_copy(zeros, app_hbm.at[r, pl.ds(i * 2, 2)], out_sem.at[r, i])

    def put(r, i):
        part = pl.ds(i * 2, 2)
        return pltpu.make_async_copy(deliv_hbm.at[r, part], app_hbm.at[r, part], out_sem.at[r, i])

    zeros[...] = jnp.zeros_like(zeros)
    for r in range(REQ):
        mine = owner_ref[t * REQ + r] == s

        @pl.when(mine)
        def _():
            for i in range(4):
                put(r, i).start()

        @pl.when(jnp.logical_not(mine))
        def _():
            for i in range(4):
                blank(r, i).start()

    for copy in small:
        copy.wait()
    for r in range(REQ):
        for i in range(4):
            put(r, i).wait()


def store(owner, residual_out, normed, delivered):
    anywhere = pl.BlockSpec(memory_space=pl.ANY)
    smem = pl.BlockSpec(memory_space=pltpu.SMEM)
    return pl.pallas_call(
        store_kernel,
        out_shape=tuple(jax.ShapeDtypeStruct(v.shape, v.dtype) for v in (residual_out, normed, delivered)),
        in_specs=[smem] + [anywhere] * 3,
        out_specs=(anywhere,) * 3,
        scratch_shapes=[
            pltpu.VMEM((2, WIDTH, 256), jnp.bfloat16),
            pltpu.SemaphoreType.DMA((REQ, 4)),
            pltpu.SemaphoreType.DMA((2,)),
        ],
        compiler_params=pltpu.CompilerParams(vmem_limit_bytes=62 * 1024 * 1024),
        cost_estimate=pl.CostEstimate(flops=0, bytes_accessed=6_000_000, transcendentals=0),
    )(owner, residual_out, normed, delivered)


def per_device(queries, cache_kv, new_kv, ctx_len, new_len, owner, wo, hidden_in, norm_gain):
    residual_out, normed, delivered = step(
        queries, cache_kv, new_kv, ctx_len, new_len, wo, hidden_in, norm_gain
    )
    return store(owner, residual_out, normed, delivered)


def solution(mesh):
    in_specs = (
        P("tp", None, None, None),
        P("tp", None, "seq", None),
        P("tp", None, "seq", None),
        P(),
        P(),
        P(),
        P(("seq", "tp"), None),
        P(None, ("seq", "tp")),
        P(("seq", "tp")),
    )
    out_specs = (P(None, ("seq", "tp")), P(None, ("seq", "tp")), P("tp", None, "seq", None))
    return jax.shard_map(
        per_device, mesh=mesh, in_specs=in_specs, out_specs=out_specs, check_vma=False
    )
```

time: 64.4 us -> 145 us (2.25)
  the two profiles are of different devices: /device:TPU:1 before, /device:TPU:103 now
where the time goes in v3:
time: 145 us; the launch traced here: 144 us
  Pallas kernels  144 us (99%)
    pallas_call x1, Pallas kernels, store(): pl.pallas_call(store_kernel, out_shape=tuple((jax.ShapeDtypeStruct(v.shap...  98.2 us
    pallas_call x1, Pallas kernels, step(): pl.pallas_call(kernel, out_shape=(jax.ShapeDtypeStruct((64, 128), bf), ja...  45.6 us

profile of v3, /device:TPU:103, one launch (start us, length us, event | category | flops | bytes accessed | tf_op | source)
XLA Modules:
  0.0 144.5 jit_solution(4224201465632043467)
XLA Ops:
  0.6 45.6 %shard_map.112 = (bf16[64,128]{1,0:T(8,128)(2,1)}, bf16[64,128]{1,0:T(8,128)(2,1)}, bf16[4,8,256,256]{3,2,1,0:T(8,128)(2,1)}) custom-call(s32[64]{0:T(128)} %ctx_hbm.1, s32[64]{0:T(128)} %new_hbm.1, bf16[4,8,16,128]{3,2,1,0:T(8,128)(2,1)} %q_hbm.1, bf16[4,8,256,256]{3,2,1,0:T(8,128)(2,1)} %cache_hbm.1, bf16[4,8,32,256]{3,2,1,0:T(8,128)(2,1)} %newkv_hbm.1, ...), custom_call_target="tpu_custom_call" | custom-call | flops 600000000 | bytes 14000000 | tf_op jit(solution)/shard_map/pallas_call | solution.py:452
  46.3 98.2 %shard_map.113 = (bf16[64,128]{1,0:T(8,128)(2,1)}, bf16[64,128]{1,0:T(8,128)(2,1)}, bf16[4,8,256,256]{3,2,1,0:T(8,128)(2,1)}) custom-call(s32[64]{0:T(128)} %owner_ref.1, bf16[64,128]{1,0:T(8,128)(2,1)} %get-tuple-element.6.res_in, bf16[64,128]{1,0:T(8,128)(2,1)} %get-tuple-element.7.norm_in, bf16[4,8,256,256]{3,2,1,0:T(8,128)(2,1)} %get-tuple-element.8.deliv_hbm), custom_call_target="tpu_custom_call" | custom-call | bytes 6000000 | tf_op jit(solution)/shard_map/pallas_call | solution.py:530

commit v4 on v3

--- a/solution.py
+++ b/solution.py
@@ -28,7 +28,7 @@
 def kernel(
     ctx_hbm, new_hbm, q_hbm, cache_hbm, newkv_hbm, wo_hbm, hidden_hbm, gain_hbm,
     res_hbm, norm_hbm, deliv_hbm,
-    ctx_s, new_s, q_v, kv, fresh, w_v, hid_v, gain_v,
+    ctx_s, new_s, q_v, kv, got, w_v, hid_v, gain_v,
     osend, orecv, csend, crecv,
     a_send, b_send, a_recv, b_recv, a2_send, b2_send, a2_recv, b2_recv,
     n_send, n_recv, rows_v, res_v, norm_v,
@@ -45,14 +45,14 @@
     sp = y * 2 + (1 - c)
 
     def seq_peer(i):
-        return lax.rem(s + 1 + i, 8)
+        return (s + 1 + i) & 7
 
     def tp_peer(i):
-        return lax.rem(t + 1 + i, 16)
+        return (t + 1 + i) & 15
 
     def any_peer(i):
-        k = lax.rem(me + 1 + i, 128)
-        return k // 16, lax.rem(k, 16)
+        k = (me + 1 + i) & 127
+        return k >> 4, k & 15
 
     def y_at(d):
         return lax.rem(y + d, 4) * 2 + c
@@ -112,19 +112,14 @@
         w_local(j).start()
 
     def block(half, who):
-        return deliv_hbm.at[pl.ds(half * 2, 2), :, pl.ds(pl.multiple_of(who * SHARE, SHARE), SHARE), :]
-
-    own = [
-        pltpu.make_async_copy(fresh.at[pl.ds(half * 2, 2)], block(half, s), gl_sem.at[half])
-        for half in range(2)
-    ]
+        return got.at[pl.ds(half * 2, 2), :, pl.ds(pl.multiple_of(who * SHARE, SHARE), SHARE), :]
 
     def ring(way, slot, src, dst):
         return remote(src, dst, gs_sem.at[way, slot], gr_sem.at[way, slot], (y_at(1 if way == 0 else 3), t))
 
     def first(way, order):
         half = order if way == 0 else 1 - order
-        return ring(way, order, fresh.at[pl.ds(half * 2, 2)], block(half, s))
+        return ring(way, order, block(half, s), block(half, s))
 
     def second(way):
         who = y_at(3) if way == 0 else y_at(1)
@@ -134,7 +129,7 @@
         return remote(src, block(half, who), ps_sem.at[slot], pr_sem.at[slot], (sp, t))
 
     def pair_own(half):
-        return pair(half, fresh.at[pl.ds(half * 2, 2)], half, s)
+        return pair(half, block(half, s), half, s)
 
     def pair_near(way, order):
         half = order if way == 0 else 1 - order
@@ -229,11 +224,18 @@
     for r in range(REQ):
         live = slot < new_s[t * REQ + r] - s * SHARE
         for h in range(KVH):
-            fresh[r, h] = jnp.where(live, kv[r, h, WIDTH:, :], jnp.zeros((), jnp.bfloat16))
+            got[r, h, pl.ds(pl.multiple_of(s * SHARE, SHARE), SHARE), :] = jnp.where(
+                live, kv[r, h, WIDTH:, :], jnp.zeros((), jnp.bfloat16)
+            )
+
+    for order in range(2):
+        for way in range(2):
+            first(way, order).start()
+    for half in range(2):
+        pair_own(half).start()
 
     def drain_gather():
         for half in range(2):
-            own[half].wait()
             pair_own(half).wait()
             for way in range(2):
                 first(way, half).wait_send()
@@ -241,6 +243,7 @@
         for way in range(2):
             second(way).wait_send()
             pair_far(way).wait()
+        pltpu.make_async_copy(got, deliv_hbm, gl_sem.at[0]).start()
 
     def drain_w():
         for j in range(4):
@@ -251,12 +254,6 @@
 
     wait_o(0)
     wait_o(1)
-    for order in range(2):
-        for way in range(2):
-            first(way, order).start()
-    for half in range(2):
-        own[half].start()
-        pair_own(half).start()
 
     tops = []
     for k in range(8):
@@ -297,6 +294,10 @@
         w_remote(j).wait_recv()
     pltpu.make_async_copy(crecv, crecv, cr_sem.at[0]).wait()
 
+    for way in range(2):
+        first(way, 0).wait_recv()
+        second(way).start()
+        pair_near(way, 0).start()
     flat = jnp.concatenate(
         [
             jnp.concatenate([crecv[core, :, r, :] for r in range(REQ)], axis=0)
@@ -307,8 +308,8 @@
 
     def r1_copy(way, d, part):
         dst = lax.rem((x if way == 0 else z) + d, 4)
-        src = (a_send if way == 0 else b_send).at[dst, pl.ds(part * 2, 2)]
-        to = (a_recv if way == 0 else b_recv).at[d - 1, pl.ds(part * 2, 2)]
+        src = (a_send if way == 0 else b_send).at[dst, part]
+        to = (a_recv if way == 0 else b_recv).at[d - 1, part]
         return remote(
             src, to, r1s_sem.at[way, d - 1, part], r1r_sem.at[way, d - 1, part],
             (s, x_at(d) if way == 0 else z_at(d)),
@@ -326,15 +327,19 @@
     def drain_r1():
         for way in range(2):
             for d in range(1, 4):
-                for part in range(2):
+                for part in range(4):
                     r1_copy(way, d, part).wait_send()
 
     drains.append(drain_r1)
-    for part in range(2):
-        lax.fori_loop(part * 2, part * 2 + 2, project, 0)
+    for part in range(4):
+        project(part, 0)
         for d in (2, 1, 3):
             for way in range(2):
                 r1_copy(way, d, part).start()
+
+    for way in range(2):
+        first(way, 1).wait_recv()
+        pair_near(way, 1).start()
 
     def r2_copy(way, j, k):
         there = z if way == 0 else x
@@ -351,7 +356,7 @@
                 pltpu.make_async_copy(sent, sent, r2s_sem.at[way]).wait()
 
     drains.append(drain_r2)
-    for part in range(2):
+    for part in range(4):
         for way in range(2):
             for d in (1, 3, 2):
                 r1_copy(way, d, part).wait_recv()
@@ -379,20 +384,12 @@
                         pltpu.make_async_copy(nxt.at[j, k], last[1].at[j, k], r2r_sem.at[way]).start()
                 return 0
 
-            lax.fori_loop(part * 2, part * 2 + 2, add, 0)
-        if part == 0:
-            for way in range(2):
-                first(way, 0).wait_recv()
-                second(way).start()
-                pair_near(way, 0).start()
+            add(part, 0)
 
     for load in loads[3:]:
         load.wait()
     rows_v[...] = hid_v[...].astype(jnp.float32)
     stream = jnp.concatenate([rows_v[pl.ds(r, 16, stride=REQ), :] for r in range(REQ)], axis=0)
-    for way in range(2):
-        first(way, 1).wait_recv()
-        pair_near(way, 1).start()
     sums = []
     for way in range(2):
         recv = (a2_recv, b2_recv)[way]
@@ -417,7 +414,6 @@
         sent = n_recv.at[pl.ds(0, 127)]
         pltpu.make_async_copy(sent, sent, ns_sem.at[0]).wait()
 
-    drains.append(drain_n)
     lax.fori_loop(0, 127, send_n, 0)
     pltpu.make_async_copy(n_send, n_recv.at[me], nr_sem.at[0]).start()
     for r in range(REQ):
@@ -429,6 +425,8 @@
         second(way).wait_recv()
         pair_far(way).start()
     scaled = stream * gain_v[...]
+    for drain in drains:
+        drain()
     pltpu.make_async_copy(n_recv, n_recv, nr_sem.at[0]).wait()
     scale = lax.rsqrt(jnp.sum(n_recv[...], axis=0) / D + 1e-05)
     scale = jnp.broadcast_to(scale, (128, 128)).T[:64]
@@ -439,9 +437,9 @@
     norm_out = pltpu.make_async_copy(norm_v, norm_hbm, out_sem.at[1])
     norm_out.start()
     res_out.wait()
+    drain_n()
+    pltpu.make_async_copy(got, deliv_hbm, gl_sem.at[0]).wait()
     norm_out.wait()
-    for drain in drains:
-        drain()
 
 
 def step(queries, cache_kv, new_kv, ctx_len, new_len, wo, hidden_in, norm_gain):
@@ -462,7 +460,7 @@
             pltpu.SMEM((64,), jnp.int32), pltpu.SMEM((64,), jnp.int32),
             V((REQ, KVH, GROUP, HD), bf),
             V((REQ, KVH, KEYS, 256), bf),
-            V((REQ, KVH, SHARE, 256), bf),
+            V((REQ, KVH, WIDTH, 256), bf),
             V((4, 256, 2048), bf),
             V((64, 128), bf),
             V((1, 128), f32),
@@ -476,8 +474,8 @@
             V((64, 128), f32), V((64, 128), bf), V((64, 128), bf),
             dma((5,)), dma((2,)), dma((REQ, 2)), dma((4,)), dma((4,)), dma((4,)),
             dma((2,)), dma((2,)), dma((1,)), dma((1,)),
-            dma((2, 3, 2)), dma((2, 3, 2)), dma((2,)), dma((2,)), dma((1,)), dma((1,)),
-            dma((2, 3)), dma((2, 3)), dma((8,)), dma((8,)), dma((2,)),
+            dma((2, 3, 4)), dma((2, 3, 4)), dma((2,)), dma((2,)), dma((1,)), dma((1,)),
+            dma((2, 3)), dma((2, 3)), dma((8,)), dma((8,)), dma((1,)),
         ],
         compiler_params=pltpu.CompilerParams(
             collective_id=0, has_side_effects=True, vmem_limit_bytes=62 * 1024 * 1024
@@ -486,37 +484,56 @@
     )(ctx_len, new_len, queries, cache_kv, new_kv, wo, hidden_in, norm_gain.reshape(1, 128))
 
 
-def store_kernel(owner_ref, res_in, norm_in, deliv_hbm, res_hbm, norm_hbm, app_hbm, zeros, out_sem, sem):
+def store_kernel(
+    owner_hbm, res_in, norm_in, deliv_hbm, res_hbm, norm_hbm, app_hbm,
+    owner_ref, zeros, held, out_sem, in_sem, sem,
+):
     s = lax.axis_index("seq")
     t = lax.axis_index("tp")
+
+    def blank(r, i):
+        return pltpu.make_async_copy(zeros, app_hbm.at[r, pl.ds(i * 2, 2)], out_sem.at[r, i])
+
+    def fetch(r, i):
+        part = pl.ds(i * 2, 2)
+        return pltpu.make_async_copy(deliv_hbm.at[r, part], held.at[r, part], in_sem.at[r, i])
+
+    def put(r, i):
+        part = pl.ds(i * 2, 2)
+        return pltpu.make_async_copy(held.at[r, part], app_hbm.at[r, part], out_sem.at[r, i])
+
+    def mine(r):
+        return owner_ref[t * REQ + r] == s
+
+    who = pltpu.make_async_copy(owner_hbm, owner_ref, sem.at[2])
+    who.start()
     small = (
         pltpu.make_async_copy(res_in, res_hbm, sem.at[0]),
         pltpu.make_async_copy(norm_in, norm_hbm, sem.at[1]),
     )
     for copy in small:
         copy.start()
-
-    def blank(r, i):
-        return pltpu.make_async_copy(zeros, app_hbm.at[r, pl.ds(i * 2, 2)], out_sem.at[r, i])
-
-    def put(r, i):
-        part = pl.ds(i * 2, 2)
-        return pltpu.make_async_copy(deliv_hbm.at[r, part], app_hbm.at[r, part], out_sem.at[r, i])
-
     zeros[...] = jnp.zeros_like(zeros)
-    for r in range(REQ):
-        mine = owner_ref[t * REQ + r] == s
-
-        @pl.when(mine)
+    who.wait()
+    for r in range(REQ):
+        @pl.when(mine(r))
         def _():
             for i in range(4):
-                put(r, i).start()
-
-        @pl.when(jnp.logical_not(mine))
+                fetch(r, i).start()
+
+    for r in range(REQ):
+        @pl.when(jnp.logical_not(mine(r)))
         def _():
             for i in range(4):
                 blank(r, i).start()
 
+    for r in range(REQ):
+        @pl.when(mine(r))
+        def _():
+            for i in range(4):
+                fetch(r, i).wait()
+                put(r, i).start()
+
     for copy in small:
         copy.wait()
     for r in range(REQ):
@@ -526,16 +543,18 @@
 
 def store(owner, residual_out, normed, delivered):
     anywhere = pl.BlockSpec(memory_space=pl.ANY)
-    smem = pl.BlockSpec(memory_space=pltpu.SMEM)
     return pl.pallas_call(
         store_kernel,
         out_shape=tuple(jax.ShapeDtypeStruct(v.shape, v.dtype) for v in (residual_out, normed, delivered)),
-        in_specs=[smem] + [anywhere] * 3,
+        in_specs=[anywhere] * 4,
         out_specs=(anywhere,) * 3,
         scratch_shapes=[
+            pltpu.SMEM((64,), jnp.int32),
             pltpu.VMEM((2, WIDTH, 256), jnp.bfloat16),
+            pltpu.VMEM((REQ, KVH, WIDTH, 256), jnp.bfloat16),
             pltpu.SemaphoreType.DMA((REQ, 4)),
-            pltpu.SemaphoreType.DMA((2,)),
+            pltpu.SemaphoreType.DMA((REQ, 4)),
+            pltpu.SemaphoreType.DMA((3,)),
         ],
         compiler_params=pltpu.CompilerParams(vmem_limit_bytes=62 * 1024 * 1024),
         cost_estimate=pl.CostEstimate(flops=0, bytes_accessed=6_000_000, transcendentals=0),

time: 145 us -> 48.8 us (0.34)
  the two profiles are of different devices: /device:TPU:103 before, /device:TPU:1 now
where the time goes in v4:
time: 48.8 us; the launch traced here: 48.6 us
  Pallas kernels  48 us (98%)
  between operations  0.64 us (1%)
    pallas_call x1, Pallas kernels, step(): pl.pallas_call(kernel, out_shape=(jax.ShapeDtypeStruct((64, 128), bf), ja...  45 us
    pallas_call x1, Pallas kernels, store(): pl.pallas_call(store_kernel, out_shape=tuple((jax.ShapeDtypeStruct(v.shap...  2.97 us

profile of v4, /device:TPU:1, one launch (start us, length us, event | category | flops | bytes accessed | tf_op | source)
XLA Modules:
  0.0 48.6 jit_solution(9544076098067018325)
XLA Ops:
  0.6 45.0 %shard_map.112 = (bf16[64,128]{1,0:T(8,128)(2,1)}, bf16[64,128]{1,0:T(8,128)(2,1)}, bf16[4,8,256,256]{3,2,1,0:T(8,128)(2,1)}) custom-call(s32[64]{0:T(128)} %ctx_hbm.1, s32[64]{0:T(128)} %new_hbm.1, bf16[4,8,16,128]{3,2,1,0:T(8,128)(2,1)} %q_hbm.1, bf16[4,8,256,256]{3,2,1,0:T(8,128)(2,1)} %cache_hbm.1, bf16[4,8,32,256]{3,2,1,0:T(8,128)(2,1)} %newkv_hbm.1, ...), custom_call_target="tpu_custom_call" | custom-call | flops 600000000 | bytes 14000000 | tf_op jit(solution)/shard_map/pallas_call | solution.py:450
  45.7 3.0 %shard_map.113 = (bf16[64,128]{1,0:T(8,128)(2,1)}, bf16[64,128]{1,0:T(8,128)(2,1)}, bf16[4,8,256,256]{3,2,1,0:T(8,128)(2,1)}) custom-call(s32[64]{0:T(128)} %owner_hbm.1, bf16[64,128]{1,0:T(8,128)(2,1)} %get-tuple-element.6.res_in, bf16[64,128]{1,0:T(8,128)(2,1)} %get-tuple-element.7.norm_in, bf16[4,8,256,256]{3,2,1,0:T(8,128)(2,1)} %get-tuple-element.8.deliv_hbm), custom_call_target="tpu_custom_call" | custom-call | bytes 6000000 | tf_op jit(solution)/shard_map/pallas_call | solution.py:546

commit v5 on v4

--- a/solution.py
+++ b/solution.py
@@ -27,15 +27,15 @@
 
 def kernel(
     ctx_hbm, new_hbm, q_hbm, cache_hbm, newkv_hbm, wo_hbm, hidden_hbm, gain_hbm,
-    res_hbm, norm_hbm, deliv_hbm,
-    ctx_s, new_s, q_v, kv, got, w_v, hid_v, gain_v,
+    res_ref, norm_ref, got,
+    ctx_s, new_s, q_v, kv, w_v, hid_v, gain_v,
     osend, orecv, csend, crecv,
     a_send, b_send, a_recv, b_recv, a2_send, b2_send, a2_recv, b2_recv,
-    n_send, n_recv, rows_v, res_v, norm_v,
-    loc_sem, out_sem, kv_sem, wl_sem, ws_sem, wr_sem,
+    n_send, n_recv, rows_v,
+    loc_sem, kv_sem, wl_sem, ws_sem, wr_sem,
     os_sem, or_sem, cs_sem, cr_sem,
     r1s_sem, r1r_sem, r2s_sem, r2r_sem, ns_sem, nr_sem,
-    gs_sem, gr_sem, ps_sem, pr_sem, gl_sem,
+    gs_sem, gr_sem, ps_sem, pr_sem,
 ):
     s = lax.axis_index("seq")
     t = lax.axis_index("tp")
@@ -48,11 +48,12 @@
         return (s + 1 + i) & 7
 
     def tp_peer(i):
-        return (t + 1 + i) & 15
+        return ((x + 2 - (i & 3)) & 3) * 4 + ((z + 2 - (i >> 2)) & 3)
 
     def any_peer(i):
-        k = (me + 1 + i) & 127
-        return k >> 4, k & 15
+        far = (y + 2 - ((i >> 5) & 3)) & 3
+        core = c ^ (1 - (i & 1))
+        return far * 2 + core, ((x + 2 - ((i >> 1) & 3)) & 3) * 4 + ((z + 2 - ((i >> 3) & 3)) & 3)
 
     def y_at(d):
         return lax.rem(y + d, 4) * 2 + c
@@ -64,6 +65,10 @@
         return x * 4 + lax.rem(z + d, 4)
 
     drains = []
+
+    def others(count, own, send):
+        lax.fori_loop(0, own, send, 0)
+        lax.fori_loop(own + 1, count, send, 0)
 
     loads = [
         pltpu.make_async_copy(src, dst, loc_sem.at[i])
@@ -92,7 +97,7 @@
         pl.semaphore_signal(barrier, inc=1, device_id=any_peer(i), device_id_type=MESH)
         return 0
 
-    lax.fori_loop(0, 127, greet, 0)
+    others(128, 85, greet)
 
     def w_local(j):
         return pltpu.make_async_copy(
@@ -243,7 +248,6 @@
         for way in range(2):
             second(way).wait_send()
             pair_far(way).wait()
-        pltpu.make_async_copy(got, deliv_hbm, gl_sem.at[0]).start()
 
     def drain_w():
         for j in range(4):
@@ -286,7 +290,7 @@
             pltpu.make_async_copy(sent, sent, cs_sem.at[0]).wait()
 
     drains.append(drain_c)
-    lax.fori_loop(0, 15, send_c, 0)
+    others(16, 10, send_c)
     c_copy(1 - c, t).start()
     pltpu.make_async_copy(csend.at[t], crecv.at[c, t], cr_sem.at[0]).start()
     for j in range(4):
@@ -414,13 +418,11 @@
         sent = n_recv.at[pl.ds(0, 127)]
         pltpu.make_async_copy(sent, sent, ns_sem.at[0]).wait()
 
-    lax.fori_loop(0, 127, send_n, 0)
+    others(128, 85, send_n)
     pltpu.make_async_copy(n_send, n_recv.at[me], nr_sem.at[0]).start()
     for r in range(REQ):
         rows_v[pl.ds(r, 16, stride=REQ), :] = stream[r * 16:(r + 1) * 16]
-    res_v[...] = rows_v[...].astype(jnp.bfloat16)
-    res_out = pltpu.make_async_copy(res_v, res_hbm, out_sem.at[0])
-    res_out.start()
+    res_ref[...] = rows_v[...].astype(jnp.bfloat16)
     for way in range(2):
         second(way).wait_recv()
         pair_far(way).start()
@@ -433,34 +435,29 @@
     normed = scaled * scale
     for r in range(REQ):
         rows_v[pl.ds(r, 16, stride=REQ), :] = normed[r * 16:(r + 1) * 16]
-    norm_v[...] = rows_v[...].astype(jnp.bfloat16)
-    norm_out = pltpu.make_async_copy(norm_v, norm_hbm, out_sem.at[1])
-    norm_out.start()
-    res_out.wait()
+    norm_ref[...] = rows_v[...].astype(jnp.bfloat16)
     drain_n()
-    pltpu.make_async_copy(got, deliv_hbm, gl_sem.at[0]).wait()
-    norm_out.wait()
 
 
 def step(queries, cache_kv, new_kv, ctx_len, new_len, wo, hidden_in, norm_gain):
     bf, f32 = jnp.bfloat16, jnp.float32
     dma = pltpu.SemaphoreType.DMA
     anywhere = pl.BlockSpec(memory_space=pl.ANY)
+    vmem = pl.BlockSpec(memory_space=pltpu.VMEM)
     V = pltpu.VMEM
     return pl.pallas_call(
         kernel,
         out_shape=(
-            jax.ShapeDtypeStruct((64, 128), bf),
-            jax.ShapeDtypeStruct((64, 128), bf),
-            jax.ShapeDtypeStruct((REQ, KVH, WIDTH, 256), bf),
+            V((64, 128), bf),
+            V((64, 128), bf),
+            V((REQ, KVH, WIDTH, 256), bf),
         ),
         in_specs=[anywhere] * 8,
-        out_specs=(anywhere, anywhere, anywhere),
+        out_specs=(vmem, vmem, vmem),
         scratch_shapes=[
             pltpu.SMEM((64,), jnp.int32), pltpu.SMEM((64,), jnp.int32),
             V((REQ, KVH, GROUP, HD), bf),
             V((REQ, KVH, KEYS, 256), bf),
-            V((REQ, KVH, WIDTH, 256), bf),
             V((4, 256, 2048), bf),
             V((64, 128), bf),
             V((1, 128), f32),
@@ -471,22 +468,27 @@
             V((4, 4, 32, 128), bf), V((4, 4, 32, 128), bf),
             V((4, 4, 32, 128), bf), V((4, 4, 32, 128), bf),
             V((1, 128), f32), V((128, 1, 128), f32),
-            V((64, 128), f32), V((64, 128), bf), V((64, 128), bf),
-            dma((5,)), dma((2,)), dma((REQ, 2)), dma((4,)), dma((4,)), dma((4,)),
+            V((64, 128), f32),
+            dma((5,)), dma((REQ, 2)), dma((4,)), dma((4,)), dma((4,)),
             dma((2,)), dma((2,)), dma((1,)), dma((1,)),
             dma((2, 3, 4)), dma((2, 3, 4)), dma((2,)), dma((2,)), dma((1,)), dma((1,)),
-            dma((2, 3)), dma((2, 3)), dma((8,)), dma((8,)), dma((1,)),
+            dma((2, 3)), dma((2, 3)), dma((8,)), dma((8,)),
         ],
         compiler_params=pltpu.CompilerParams(
-            collective_id=0, has_side_effects=True, vmem_limit_bytes=62 * 1024 * 1024
+            collective_id=0, has_side_effects=True, vmem_limit_bytes=40 * 1024 * 1024
         ),
         cost_estimate=pl.CostEstimate(flops=600_000_000, bytes_accessed=14_000_000, transcendentals=1_000_000),
-    )(ctx_len, new_len, queries, cache_kv, new_kv, wo, hidden_in, norm_gain.reshape(1, 128))
+    )(
+        *(
+            pltpu.with_memory_space_constraint(v, pltpu.HBM)
+            for v in (ctx_len, new_len, queries, cache_kv, new_kv, wo, hidden_in, norm_gain.reshape(1, 128))
+        )
+    )
 
 
 def store_kernel(
-    owner_hbm, res_in, norm_in, deliv_hbm, res_hbm, norm_hbm, app_hbm,
-    owner_ref, zeros, held, out_sem, in_sem, sem,
+    owner_hbm, res_in, norm_in, deliv_ref, res_hbm, norm_hbm, app_hbm,
+    owner_ref, zeros, out_sem, sem,
 ):
     s = lax.axis_index("seq")
     t = lax.axis_index("tp")
@@ -494,13 +496,9 @@
     def blank(r, i):
         return pltpu.make_async_copy(zeros, app_hbm.at[r, pl.ds(i * 2, 2)], out_sem.at[r, i])
 
-    def fetch(r, i):
-        part = pl.ds(i * 2, 2)
-        return pltpu.make_async_copy(deliv_hbm.at[r, part], held.at[r, part], in_sem.at[r, i])
-
     def put(r, i):
         part = pl.ds(i * 2, 2)
-        return pltpu.make_async_copy(held.at[r, part], app_hbm.at[r, part], out_sem.at[r, i])
+        return pltpu.make_async_copy(deliv_ref.at[r, part], app_hbm.at[r, part], out_sem.at[r, i])
 
     def mine(r):
         return owner_ref[t * REQ + r] == s
@@ -519,7 +517,7 @@
         @pl.when(mine(r))
         def _():
             for i in range(4):
-                fetch(r, i).start()
+                put(r, i).start()
 
     for r in range(REQ):
         @pl.when(jnp.logical_not(mine(r)))
@@ -527,13 +525,6 @@
             for i in range(4):
                 blank(r, i).start()
 
-    for r in range(REQ):
-        @pl.when(mine(r))
-        def _():
-            for i in range(4):
-                fetch(r, i).wait()
-                put(r, i).start()
-
     for copy in small:
         copy.wait()
     for r in range(REQ):
@@ -543,22 +534,24 @@
 
 def store(owner, residual_out, normed, delivered):
     anywhere = pl.BlockSpec(memory_space=pl.ANY)
+    vmem = pl.BlockSpec(memory_space=pltpu.VMEM)
     return pl.pallas_call(
         store_kernel,
         out_shape=tuple(jax.ShapeDtypeStruct(v.shape, v.dtype) for v in (residual_out, normed, delivered)),
-        in_specs=[anywhere] * 4,
+        in_specs=[anywhere] + [vmem] * 3,
         out_specs=(anywhere,) * 3,
         scratch_shapes=[
             pltpu.SMEM((64,), jnp.int32),
             pltpu.VMEM((2, WIDTH, 256), jnp.bfloat16),
-            pltpu.VMEM((REQ, KVH, WIDTH, 256), jnp.bfloat16),
-            pltpu.SemaphoreType.DMA((REQ, 4)),
             pltpu.SemaphoreType.DMA((REQ, 4)),
             pltpu.SemaphoreType.DMA((3,)),
         ],
-        compiler_params=pltpu.CompilerParams(vmem_limit_bytes=62 * 1024 * 1024),
+        compiler_params=pltpu.CompilerParams(vmem_limit_bytes=20 * 1024 * 1024),
         cost_estimate=pl.CostEstimate(flops=0, bytes_accessed=6_000_000, transcendentals=0),
-    )(owner, residual_out, normed, delivered)
+    )(
+        pltpu.with_memory_space_constraint(owner, pltpu.HBM),
+        *(pltpu.with_memory_space_constraint(v, pltpu.VMEM) for v in (residual_out, normed, delivered)),
+    )
 
 
 def per_device(queries, cache_kv, new_kv, ctx_len, new_len, owner, wo, hidden_in, norm_gain):

time: 48.8 us -> 47.6 us (0.975)
  Pallas kernels: 48 us -> 46.8 us
    pallas_call x1, Pallas kernels: 45 us -> 44 us  [step(): pl.pallas_call(kernel, out_shape=(V((64, 128), bf), V((64, 128), bf), V((...]
where the time goes in v5:
time: 47.6 us; the launch traced here: 47.5 us
  Pallas kernels  46.8 us (98%)
  between operations  0.64 us (1%)
    pallas_call x1, Pallas kernels, step(): pl.pallas_call(kernel, out_shape=(V((64, 128), bf), V((64, 128), bf), V((...  44 us
    pallas_call x1, Pallas kernels, store(): pl.pallas_call(store_kernel, out_shape=tuple((jax.ShapeDtypeStruct(v.shap...  2.85 us

profile of v5, /device:TPU:1, one launch (start us, length us, event | category | flops | bytes accessed | tf_op | source)
XLA Modules:
  0.0 47.5 jit_solution(16048063854574508013)
XLA Ops:
  0.6 44.0 %shard_map.112 = (bf16[64,128]{1,0:T(8,128)(2,1)S(1)}, bf16[64,128]{1,0:T(8,128)(2,1)S(1)}, bf16[4,8,256,256]{3,2,1,0:T(8,128)(2,1)S(1)}) custom-call(s32[64]{0:T(128)} %ctx_hbm.1, s32[64]{0:T(128)} %new_hbm.1, bf16[4,8,16,128]{3,2,1,0:T(8,128)(2,1)} %q_hbm.1, bf16[4,8,256,256]{3,2,1,0:T(8,128)(2,1)} %cache_hbm.1, bf16[4,8,32,256]{3,2,1,0:T(8,128)(2,1)} %newkv_hbm.1, ...), custom_call_target="tpu_custom_call" | custom-call | flops 600000000 | bytes 14000000 | tf_op jit(solution)/shard_map/pallas_call | solution.py:448
  44.6 2.8 %shard_map.113 = (bf16[64,128]{1,0:T(8,128)(2,1)}, bf16[64,128]{1,0:T(8,128)(2,1)}, bf16[4,8,256,256]{3,2,1,0:T(8,128)(2,1)}) custom-call(s32[64]{0:T(128)} %owner_hbm.1, bf16[64,128]{1,0:T(8,128)(2,1)S(1)} %get-tuple-element.6.res_in, bf16[64,128]{1,0:T(8,128)(2,1)S(1)} %get-tuple-element.7.norm_in, bf16[4,8,256,256]{3,2,1,0:T(8,128)(2,1)S(1)} %get-tuple-element.8.deliv_ref), custom_call_target="tpu_custom_call" | custom-call | bytes 6000000 | tf_op jit(solution)/shard_map/pallas_call | solution.py:538

commit v6 on v5

--- a/solution.py
+++ b/solution.py
@@ -30,11 +30,11 @@
     res_ref, norm_ref, got,
     ctx_s, new_s, q_v, kv, w_v, hid_v, gain_v,
     osend, orecv, csend, crecv,
-    a_send, b_send, a_recv, b_recv, a2_send, b2_send, a2_recv, b2_recv,
+    a_send, b_send, e_send, a_recv, b_recv, e_recv, a2_send, b2_send, e2_send, a2_recv, b2_recv, e2_recv,
     n_send, n_recv, rows_v,
     loc_sem, kv_sem, wl_sem, ws_sem, wr_sem,
     os_sem, or_sem, cs_sem, cr_sem,
-    r1s_sem, r1r_sem, r2s_sem, r2r_sem, ns_sem, nr_sem,
+    r1s_sem, r1r_sem, e1s_sem, e1r_sem, r2s_sem, r2r_sem, ns_sem, nr_sem,
     gs_sem, gr_sem, ps_sem, pr_sem,
 ):
     s = lax.axis_index("seq")
@@ -116,33 +116,63 @@
     for j in range(4):
         w_local(j).start()
 
-    def block(half, who):
-        return got.at[pl.ds(half * 2, 2), :, pl.ds(pl.multiple_of(who * SHARE, SHARE), SHARE), :]
-
-    def ring(way, slot, src, dst):
-        return remote(src, dst, gs_sem.at[way, slot], gr_sem.at[way, slot], (y_at(1 if way == 0 else 3), t))
-
-    def first(way, order):
-        half = order if way == 0 else 1 - order
-        return ring(way, order, block(half, s), block(half, s))
-
-    def second(way):
-        who = y_at(3) if way == 0 else y_at(1)
-        return ring(way, 2, block(way, who), block(way, who))
-
-    def pair(slot, src, half, who):
-        return remote(src, block(half, who), ps_sem.at[slot], pr_sem.at[slot], (sp, t))
-
-    def pair_own(half):
-        return pair(half, block(half, s), half, s)
-
-    def pair_near(way, order):
-        half = order if way == 0 else 1 - order
-        who = y_at(3) if way == 0 else y_at(1)
-        return pair(2 + way * 2 + order, block(half, who), half, who)
-
-    def pair_far(way):
-        return pair(6 + way, block(way, y_at(2)), way, y_at(2))
+    def block(r, who):
+        return got.at[r, :, pl.ds(pl.multiple_of(who * SHARE, SHARE), SHARE), :]
+
+    def request(way, n):
+        return n if way == 0 else REQ - 1 - n
+
+    def source(way):
+        return y_at(3 if way == 0 else 1)
+
+    def ring(way, n, slot, who):
+        here = block(request(way, n), who)
+        return remote(
+            here, here, gs_sem.at[way, slot], gr_sem.at[way, slot], (y_at(1 if way == 0 else 3), t)
+        )
+
+    def first(way, n):
+        return ring(way, n, n, s)
+
+    def second(way, n):
+        return ring(way, n, REQ + n, source(way))
+
+    def pair(way, n, slot, who):
+        here = block(request(way, n), who)
+        return remote(here, here, ps_sem.at[way, slot], pr_sem.at[way, slot], (sp, t))
+
+    def pair_own(n):
+        return pair(0, n, n, s)
+
+    def pair_near(way, n):
+        return pair(way, n, REQ + n, source(way))
+
+    def pair_far(way, n):
+        return pair(way, n, 2 * REQ + n, y_at(2))
+
+    def start_first(*steps):
+        for n in steps:
+            for way in range(2):
+                first(way, n).start()
+
+    def start_second(*steps):
+        for n in steps:
+            for way in range(2):
+                first(way, n).wait_recv()
+                second(way, n).start()
+                pair_near(way, n).start()
+
+    def start_near(*steps):
+        for n in steps:
+            for way in range(2):
+                first(way, n).wait_recv()
+                pair_near(way, n).start()
+
+    def start_far():
+        for n in range(2):
+            for way in range(2):
+                second(way, n).wait_recv()
+                pair_far(way, n).start()
 
     col = lax.broadcasted_iota(jnp.int32, (KVH * GROUP, KEYS), 1)
     lane = lax.broadcasted_iota(jnp.int32, (KVH * GROUP, 128), 1)
@@ -233,21 +263,19 @@
                 live, kv[r, h, WIDTH:, :], jnp.zeros((), jnp.bfloat16)
             )
 
-    for order in range(2):
-        for way in range(2):
-            first(way, order).start()
-    for half in range(2):
-        pair_own(half).start()
+    start_first(0, 1, 2)
+    for n in range(REQ):
+        pair_own(n).start()
 
     def drain_gather():
-        for half in range(2):
-            pair_own(half).wait()
+        for n in range(REQ):
+            pair_own(n).wait()
             for way in range(2):
-                first(way, half).wait_send()
-                pair_near(way, half).wait()
-        for way in range(2):
-            second(way).wait_send()
-            pair_far(way).wait()
+                first(way, n).wait_send()
+                pair_near(way, n).wait()
+                if n < 2:
+                    second(way, n).wait_send()
+                    pair_far(way, n).wait()
 
     def drain_w():
         for j in range(4):
@@ -298,10 +326,6 @@
         w_remote(j).wait_recv()
     pltpu.make_async_copy(crecv, crecv, cr_sem.at[0]).wait()
 
-    for way in range(2):
-        first(way, 0).wait_recv()
-        second(way).start()
-        pair_near(way, 0).start()
     flat = jnp.concatenate(
         [
             jnp.concatenate([crecv[core, :, r, :] for r in range(REQ)], axis=0)
@@ -311,7 +335,7 @@
     ).astype(jnp.bfloat16)
 
     def r1_copy(way, d, part):
-        dst = lax.rem((x if way == 0 else z) + d, 4)
+        dst = ((x if way == 0 else z) + d) & 3
         src = (a_send if way == 0 else b_send).at[dst, part]
         to = (a_recv if way == 0 else b_recv).at[d - 1, part]
         return remote(
@@ -319,84 +343,109 @@
             (s, x_at(d) if way == 0 else z_at(d)),
         )
 
-    def project(j, _):
+    def e1_copy(d):
+        return remote(
+            e_send.at[(y + d) & 3], e_recv.at[d - 1], e1s_sem.at[d - 1], e1r_sem.at[d - 1], (y_at(d), t)
+        )
+
+    def project(j):
         for i in range(4):
             piece = jnp.dot(flat, w_v[j, :, i * 512:(i + 1) * 512], preferred_element_type=jnp.float32)
-            piece = piece.astype(jnp.bfloat16)
-            a_send[i, j] = piece[:32]
+            a_send[i, j] = piece[:24].astype(jnp.bfloat16)
+            middle = piece[24:48].astype(jnp.bfloat16)
             for k in range(4):
-                b_send[k, j, :, i * 128:(i + 1) * 128] = piece[32:, k * 128:(k + 1) * 128]
-        return 0
+                b_send[k, j, :, i * 128:(i + 1) * 128] = middle[:, k * 128:(k + 1) * 128]
+            e_send[j, :, i * 512:(i + 1) * 512] = piece[48:].astype(jnp.bfloat16)
 
     def drain_r1():
-        for way in range(2):
-            for d in range(1, 4):
+        for d in range(1, 4):
+            e1_copy(d).wait_send()
+            for way in range(2):
                 for part in range(4):
                     r1_copy(way, d, part).wait_send()
 
     drains.append(drain_r1)
-    for part in range(4):
-        project(part, 0)
+    turns = (2, 1, 3, 0)
+    for turn in turns:
+        part = (y + turn) & 3
+        project(part)
+        if turn:
+            e1_copy(turn).start()
         for d in (2, 1, 3):
             for way in range(2):
                 r1_copy(way, d, part).start()
 
-    for way in range(2):
-        first(way, 1).wait_recv()
-        pair_near(way, 1).start()
-
+    start_first(3)
     def r2_copy(way, j, k):
-        there = z if way == 0 else x
-        send, recv = ((a2_send, a2_recv), (b2_send, b2_recv))[way]
-        return remote(
-            send.at[j, k], recv.at[y, there], r2s_sem.at[way], r2r_sem.at[way],
-            (j * 2 + c, x * 4 + k if way == 0 else k * 4 + z),
-        )
+        send, recv = ((a2_send, a2_recv), (b2_send, b2_recv), (e2_send, e2_recv))[way]
+        if way == 2:
+            slot, device = (x, z), (s, j * 4 + k)
+        else:
+            slot = (y, z if way == 0 else x)
+            device = (j * 2 + c, x * 4 + k if way == 0 else k * 4 + z)
+        return remote(send.at[j, k], recv.at[slot], r2s_sem.at[way], r2r_sem.at[way], device)
+
+    def send_r2(way, j, k):
+        send, recv = ((a2_send, a2_recv), (b2_send, b2_recv), (e2_send, e2_recv))[way]
+        mine = ((y, z), (y, x), (x, z))[way]
+        away = (j != mine[0]) | (k != mine[1])
+
+        @pl.when(away)
+        def _():
+            r2_copy(way, j, k).start()
+
+        @pl.when(jnp.logical_not(away))
+        def _():
+            pltpu.make_async_copy(send.at[j, k], recv.at[j, k], r2r_sem.at[way]).start()
 
     def drain_r2():
-        for way in range(2):
-            send = (a2_send, b2_send)[way]
+        for way in range(3):
+            send = (a2_send, b2_send, e2_send)[way]
             for sent in (send.at[pl.ds(0, 3)], send.at[0, pl.ds(0, 3)]):
                 pltpu.make_async_copy(sent, sent, r2s_sem.at[way]).wait()
 
+    def add_e():
+        for d in (1, 3, 2):
+            e1_copy(d).wait_recv()
+        for j in (2, 1, 3, 0):
+            cols = slice(j * 512, (j + 1) * 512)
+            out = e_send[y, :, cols].astype(jnp.float32)
+            for d in range(3):
+                out = out + e_recv[d, :, cols].astype(jnp.float32)
+            out = out.astype(jnp.bfloat16)
+            for k in range(4):
+                e2_send[j, k] = out[:, k * 128:(k + 1) * 128]
+            for k in range(4):
+                send_r2(2, j, k)
+
     drains.append(drain_r2)
-    for part in range(4):
+    for turn in turns:
+        part = (y + turn) & 3
         for way in range(2):
             for d in (1, 3, 2):
                 r1_copy(way, d, part).wait_recv()
             send, recv, nxt = ((a_send, a_recv, a2_send), (b_send, b_recv, b2_send))[way]
-            last = ((a2_send, a2_recv), (b2_send, b2_recv))[way]
-            mine = x if way == 0 else z
-            there = z if way == 0 else x
-
-            def add(j, _):
-                out = send[mine, j].astype(jnp.float32)
-                for d in range(3):
-                    out = out + recv[d, j].astype(jnp.float32)
-                out = out.astype(jnp.bfloat16)
-                for k in range(4):
-                    nxt[j, k] = out[:, k * 128:(k + 1) * 128]
-                for k in range(4):
-                    away = (j != y) | (k != there)
-
-                    @pl.when(away)
-                    def _():
-                        r2_copy(way, j, k).start()
-
-                    @pl.when(jnp.logical_not(away))
-                    def _():
-                        pltpu.make_async_copy(nxt.at[j, k], last[1].at[j, k], r2r_sem.at[way]).start()
-                return 0
-
-            add(part, 0)
+            out = send[x if way == 0 else z, part].astype(jnp.float32)
+            for d in range(3):
+                out = out + recv[d, part].astype(jnp.float32)
+            out = out.astype(jnp.bfloat16)
+            for k in range(4):
+                nxt[part, k] = out[:, k * 128:(k + 1) * 128]
+            for k in range(4):
+                send_r2(way, part, k)
+        if turn == 3:
+            add_e()
+
+    start_second(0, 1)
 
     for load in loads[3:]:
         load.wait()
     rows_v[...] = hid_v[...].astype(jnp.float32)
     stream = jnp.concatenate([rows_v[pl.ds(r, 16, stride=REQ), :] for r in range(REQ)], axis=0)
+    start_near(2, 3)
     sums = []
-    for way in range(2):
-        recv = (a2_recv, b2_recv)[way]
+    for way in range(3):
+        recv = (a2_recv, b2_recv, e2_recv)[way]
         pltpu.make_async_copy(recv, recv, r2r_sem.at[way]).wait()
         out = recv[0, 0].astype(jnp.float32)
         for i in range(1, 16):
@@ -423,9 +472,8 @@
     for r in range(REQ):
         rows_v[pl.ds(r, 16, stride=REQ), :] = stream[r * 16:(r + 1) * 16]
     res_ref[...] = rows_v[...].astype(jnp.bfloat16)
-    for way in range(2):
-        second(way).wait_recv()
-        pair_far(way).start()
+
+    start_far()
     scaled = stream * gain_v[...]
     for drain in drains:
         drain()
@@ -463,16 +511,16 @@
             V((1, 128), f32),
             V((8, 80, HD), bf), V((8, 80, HD), bf),
             V((16, REQ, HD), f32), V((2, 16, REQ, HD), f32),
-            V((4, 4, 32, 512), bf), V((4, 4, 32, 512), bf),
-            V((3, 4, 32, 512), bf), V((3, 4, 32, 512), bf),
-            V((4, 4, 32, 128), bf), V((4, 4, 32, 128), bf),
-            V((4, 4, 32, 128), bf), V((4, 4, 32, 128), bf),
+            V((4, 4, 24, 512), bf), V((4, 4, 24, 512), bf), V((4, 16, 2048), bf),
+            V((3, 4, 24, 512), bf), V((3, 4, 24, 512), bf), V((3, 16, 2048), bf),
+            V((4, 4, 24, 128), bf), V((4, 4, 24, 128), bf), V((4, 4, 16, 128), bf),
+            V((4, 4, 24, 128), bf), V((4, 4, 24, 128), bf), V((4, 4, 16, 128), bf),
             V((1, 128), f32), V((128, 1, 128), f32),
             V((64, 128), f32),
             dma((5,)), dma((REQ, 2)), dma((4,)), dma((4,)), dma((4,)),
             dma((2,)), dma((2,)), dma((1,)), dma((1,)),
-            dma((2, 3, 4)), dma((2, 3, 4)), dma((2,)), dma((2,)), dma((1,)), dma((1,)),
-            dma((2, 3)), dma((2, 3)), dma((8,)), dma((8,)),
+            dma((2, 3, 4)), dma((2, 3, 4)), dma((3,)), dma((3,)), dma((3,)), dma((3,)), dma((1,)), dma((1,)),
+            dma((2, 6)), dma((2, 6)), dma((2, 10)), dma((2, 10)),
         ],
         compiler_params=pltpu.CompilerParams(
             collective_id=0, has_side_effects=True, vmem_limit_bytes=40 * 1024 * 1024
@@ -549,7 +597,7 @@
         compiler_params=pltpu.CompilerParams(vmem_limit_bytes=20 * 1024 * 1024),
         cost_estimate=pl.CostEstimate(flops=0, bytes_accessed=6_000_000, transcendentals=0),
     )(
-        pltpu.with_memory_space_constraint(owner, pltpu.HBM),
+        owner,
         *(pltpu.with_memory_space_constraint(v, pltpu.VMEM) for v in (residual_out, normed, delivered)),
     )
 

time: 47.6 us -> 45.1 us (0.947)
  Pallas kernels: 46.8 us -> 44.4 us
    pallas_call x1, Pallas kernels: 44 us -> 41.6 us  [step(): pl.pallas_call(kernel, out_shape=(V((64, 128), bf), V((64, 128), bf), V((...]
where the time goes in v6:
time: 45.1 us; the launch traced here: 45 us
  Pallas kernels  44.4 us (98%)
  between operations  0.66 us (1%)
    pallas_call x1, Pallas kernels, step(): pl.pallas_call(kernel, out_shape=(V((64, 128), bf), V((64, 128), bf), V((...  41.6 us
    pallas_call x1, Pallas kernels, store(): pl.pallas_call(store_kernel, out_shape=tuple((jax.ShapeDtypeStruct(v.shap...  2.73 us

profile of v6, /device:TPU:1, one launch (start us, length us, event | category | flops | bytes accessed | tf_op | source)
XLA Modules:
  0.0 45.0 jit_solution(5511363203045456705)
XLA Ops:
  0.6 0.0 copy-start
  0.6 41.6 %shard_map.112 = (bf16[64,128]{1,0:T(8,128)(2,1)S(1)}, bf16[64,128]{1,0:T(8,128)(2,1)S(1)}, bf16[4,8,256,256]{3,2,1,0:T(8,128)(2,1)S(1)}) custom-call(s32[64]{0:T(128)} %ctx_hbm.1, s32[64]{0:T(128)} %new_hbm.1, bf16[4,8,16,128]{3,2,1,0:T(8,128)(2,1)} %q_hbm.1, bf16[4,8,256,256]{3,2,1,0:T(8,128)(2,1)} %cache_hbm.1, bf16[4,8,32,256]{3,2,1,0:T(8,128)(2,1)} %newkv_hbm.1, ...), custom_call_target="tpu_custom_call" | custom-call | flops 600000000 | bytes 14000000 | tf_op jit(solution)/shard_map/pallas_call | solution.py:496
  42.3 0.0 copy-done
  42.3 2.7 %shard_map.113 = (bf16[64,128]{1,0:T(8,128)(2,1)}, bf16[64,128]{1,0:T(8,128)(2,1)}, bf16[4,8,256,256]{3,2,1,0:T(8,128)(2,1)}) custom-call(s32[64]{0:T(128)S(1)} %copy-done, bf16[64,128]{1,0:T(8,128)(2,1)S(1)} %get-tuple-element.6.res_in, bf16[64,128]{1,0:T(8,128)(2,1)S(1)} %get-tuple-element.7.norm_in, bf16[4,8,256,256]{3,2,1,0:T(8,128)(2,1)S(1)} %get-tuple-element.8.deliv_ref), custom_call_target="tpu_custom_call" | custom-call | bytes 6000000 | tf_op jit(solution)/shard_map/pallas_call | solution.py:586
Async XLA Ops:
  0.6 41.7 %copy-start = (s32[64]{0:T(128)S(1)}, s32[64]{0:T(128)}, u32[]{:S(2)}) copy-start(s32[64]{0:T(128)} %owner_hbm.1) | copy-start | bytes 772

commit v7 on v6

--- a/solution.py
+++ b/solution.py
@@ -16,6 +16,7 @@
 SHARE = 32
 KEYS = WIDTH + SHARE
 NEG = -1e30
+LOG2E = 1.4426950408889634
 MESH = pl.DeviceIdType.MESH
 
 
@@ -70,6 +71,23 @@
         lax.fori_loop(0, own, send, 0)
         lax.fori_loop(own + 1, count, send, 0)
 
+    barrier = pltpu.get_barrier_semaphore()
+
+    def greet(device):
+        pl.semaphore_signal(barrier, inc=1, device_id=device, device_id_type=MESH)
+
+    def greet_tp(i, _):
+        greet((sp, tp_peer(i)))
+        greet((s, tp_peer(i)))
+        return 0
+
+    def greet_seq(i, _):
+        greet((seq_peer(i), t))
+        return 0
+
+    others(16, 10, greet_tp)
+    lax.fori_loop(0, 7, greet_seq, 0)
+
     loads = [
         pltpu.make_async_copy(src, dst, loc_sem.at[i])
         for i, (src, dst) in enumerate(
@@ -85,19 +103,15 @@
 
     for load in loads[:3]:
         load.start()
-    for r in range(REQ):
+    for r in range(2):
+        for copy in kv_copies(r):
+            copy.start()
+
+    for r in range(2, REQ):
         for copy in kv_copies(r):
             copy.start()
     for load in loads[3:]:
         load.start()
-
-    barrier = pltpu.get_barrier_semaphore()
-
-    def greet(i, _):
-        pl.semaphore_signal(barrier, inc=1, device_id=any_peer(i), device_id_type=MESH)
-        return 0
-
-    others(128, 85, greet)
 
     def w_local(j):
         return pltpu.make_async_copy(
@@ -174,35 +188,50 @@
                 second(way, n).wait_recv()
                 pair_far(way, n).start()
 
-    col = lax.broadcasted_iota(jnp.int32, (KVH * GROUP, KEYS), 1)
+    col = lax.broadcasted_iota(jnp.int32, (1, KEYS), 1)
     lane = lax.broadcasted_iota(jnp.int32, (KVH * GROUP, 128), 1)
 
-    def attend(r, stats):
-        for copy in kv_copies(r):
-            copy.wait()
-        live_ctx = jnp.minimum(ctx_s[t * REQ + r] - s * WIDTH, WIDTH)
-        live_new = new_s[t * REQ + r] - s * SHARE + WIDTH
-        mask = (col < live_ctx) | ((col >= WIDTH) & (col < live_new))
-        scores = jnp.concatenate(
+    def attend(pair_of, stats):
+        scores = []
+        for r in pair_of:
+            for copy in kv_copies(r):
+                copy.wait()
+        for r in pair_of:
+            live_ctx = jnp.minimum(ctx_s[t * REQ + r] - s * WIDTH, WIDTH)
+            live_new = new_s[t * REQ + r] - s * SHARE + WIDTH
+            bias = jnp.where((col < live_ctx) | ((col >= WIDTH) & (col < live_new)), 0.0, NEG)
+            for h in range(KVH):
+                scores.append(
+                    lax.dot_general(
+                        q_v[r, h], kv[r, h, :, :HD], (((1,), (1,)), ((), ())), preferred_element_type=jnp.float32
+                    )
+                    + bias
+                )
+        scores = jnp.concatenate(scores, axis=0)
+        top = jnp.maximum(jnp.max(scores, axis=1, keepdims=True), 0.1 * NEG)
+        weights = jnp.exp2((scores - top) * (HD ** (-0.5) * LOG2E))
+        total = jnp.maximum(jnp.sum(weights, axis=1, keepdims=True), 1e-30)
+        weights = weights.astype(jnp.bfloat16)
+        out = jnp.concatenate(
             [
-                lax.dot_general(
-                    q_v[r, h], kv[r, h, :, :HD], (((1,), (1,)), ((), ())), preferred_element_type=jnp.float32
+                jnp.dot(
+                    weights[(i * KVH + h) * GROUP:(i * KVH + h + 1) * GROUP],
+                    kv[r, h, :, HD:],
+                    preferred_element_type=jnp.float32,
                 )
+                for i, r in enumerate(pair_of)
                 for h in range(KVH)
             ],
             axis=0,
-        ) * HD ** (-0.5)
-        scores = jnp.where(mask, scores, NEG)
-        top = jnp.max(scores, axis=1, keepdims=True)
-        weights = jnp.where(mask, jnp.exp(scores - top), 0.0)
-        total = jnp.maximum(jnp.sum(weights, axis=1, keepdims=True), 1e-30)
-        weights = weights.astype(jnp.bfloat16)
-        inverse = 1.0 / total
-        for h in range(KVH):
-            rows = slice(h * GROUP, (h + 1) * GROUP)
-            out = jnp.dot(weights[rows], kv[r, h, :, HD:], preferred_element_type=jnp.float32)
-            osend[h, r * GROUP:(r + 1) * GROUP, :] = (out * inverse[rows]).astype(jnp.bfloat16)
-        return jnp.where(lane == r, top + jnp.log(total), stats)
+        )
+        out = (out * (1.0 / total)).astype(jnp.bfloat16)
+        log_total = top * HD ** (-0.5) + jnp.log(total)
+        for i, r in enumerate(pair_of):
+            for h in range(KVH):
+                first_row = (i * KVH + h) * GROUP
+                osend[h, r * GROUP:(r + 1) * GROUP, :] = out[first_row:first_row + GROUP]
+            stats = jnp.where(lane == r, log_total[i * KVH * GROUP:(i + 1) * KVH * GROUP], stats)
+        return stats
 
     def rows_of(part):
         return pl.ds(0, 32) if part == 0 else pl.ds(32, 48)
@@ -238,15 +267,13 @@
     for load in loads[:3]:
         load.wait()
     stats = jnp.zeros((KVH * GROUP, 128), jnp.float32)
-    stats = attend(0, stats)
-    stats = attend(1, stats)
-    pl.semaphore_wait(barrier, 127)
+    stats = attend((0, 1), stats)
+    pl.semaphore_wait(barrier, 37)
     drains.append(drain_o)
     send_o(0)
     for j in range(4):
         w_remote(j).start()
-    stats = attend(2, stats)
-    stats = attend(3, stats)
+    stats = attend((2, 3), stats)
     high = stats.astype(jnp.bfloat16).astype(jnp.float32)
     middle = (stats - high).astype(jnp.bfloat16).astype(jnp.float32)
     low = stats - high - middle

time: 45.1 us -> 42.8 us (0.949)
  Pallas kernels: 44.4 us -> 42 us
    pallas_call x1, Pallas kernels: 41.6 us -> 39.3 us  [step(): pl.pallas_call(kernel, out_shape=(V((64, 128), bf), V((64, 128), bf), V((...]
where the time goes in v7:
time: 42.8 us; the launch traced here: 42.7 us
  Pallas kernels  42 us (98%)
  between operations  0.66 us (2%)
    pallas_call x1, Pallas kernels, step(): pl.pallas_call(kernel, out_shape=(V((64, 128), bf), V((64, 128), bf), V((...  39.3 us
    pallas_call x1, Pallas kernels, store(): pl.pallas_call(store_kernel, out_shape=tuple((jax.ShapeDtypeStruct(v.shap...  2.7 us

profile of v7, /device:TPU:1, one launch (start us, length us, event | category | flops | bytes accessed | tf_op | source)
XLA Modules:
  0.0 42.7 jit_solution(6173139570068299484)
XLA Ops:
  0.6 0.0 copy-start
  0.6 39.3 %shard_map.112 = (bf16[64,128]{1,0:T(8,128)(2,1)S(1)}, bf16[64,128]{1,0:T(8,128)(2,1)S(1)}, bf16[4,8,256,256]{3,2,1,0:T(8,128)(2,1)S(1)}) custom-call(s32[64]{0:T(128)} %ctx_hbm.1, s32[64]{0:T(128)} %new_hbm.1, bf16[4,8,16,128]{3,2,1,0:T(8,128)(2,1)} %q_hbm.1, bf16[4,8,256,256]{3,2,1,0:T(8,128)(2,1)} %cache_hbm.1, bf16[4,8,32,256]{3,2,1,0:T(8,128)(2,1)} %newkv_hbm.1, ...), custom_call_target="tpu_custom_call" | custom-call | flops 600000000 | bytes 14000000 | tf_op jit(solution)/shard_map/pallas_call | solution.py:523
  40.0 0.0 copy-done
  40.0 2.7 %shard_map.113 = (bf16[64,128]{1,0:T(8,128)(2,1)}, bf16[64,128]{1,0:T(8,128)(2,1)}, bf16[4,8,256,256]{3,2,1,0:T(8,128)(2,1)}) custom-call(s32[64]{0:T(128)S(1)} %copy-done, bf16[64,128]{1,0:T(8,128)(2,1)S(1)} %get-tuple-element.6.res_in, bf16[64,128]{1,0:T(8,128)(2,1)S(1)} %get-tuple-element.7.norm_in, bf16[4,8,256,256]{3,2,1,0:T(8,128)(2,1)S(1)} %get-tuple-element.8.deliv_ref), custom_call_target="tpu_custom_call" | custom-call | bytes 6000000 | tf_op jit(solution)/shard_map/pallas_call | solution.py:613
Async XLA Ops:
  0.6 39.4 %copy-start = (s32[64]{0:T(128)S(1)}, s32[64]{0:T(128)}, u32[]{:S(2)}) copy-start(s32[64]{0:T(128)} %owner_hbm.1) | copy-start | bytes 772

commit v8 on v7

--- a/solution.py
+++ b/solution.py
@@ -27,8 +27,8 @@
 
 
 def kernel(
-    ctx_hbm, new_hbm, q_hbm, cache_hbm, newkv_hbm, wo_hbm, hidden_hbm, gain_hbm,
-    res_ref, norm_ref, got,
+    owner_hbm, ctx_hbm, new_hbm, q_hbm, cache_hbm, newkv_hbm, wo_hbm, hidden_hbm, gain_hbm,
+    res_ref, norm_ref, got, owner_out,
     ctx_s, new_s, q_v, kv, w_v, hid_v, gain_v,
     osend, orecv, csend, crecv,
     a_send, b_send, e_send, a_recv, b_recv, e_recv, a2_send, b2_send, e2_send, a2_recv, b2_recv, e2_recv,
@@ -91,7 +91,8 @@
     loads = [
         pltpu.make_async_copy(src, dst, loc_sem.at[i])
         for i, (src, dst) in enumerate(
-            [(ctx_hbm, ctx_s), (new_hbm, new_s), (q_hbm, q_v), (hidden_hbm, hid_v), (gain_hbm, gain_v)]
+            [(ctx_hbm, ctx_s), (new_hbm, new_s), (q_hbm, q_v), (hidden_hbm, hid_v), (gain_hbm, gain_v),
+             (owner_hbm, owner_out)]
         )
     ]
 
@@ -194,8 +195,7 @@
     def attend(pair_of, stats):
         scores = []
         for r in pair_of:
-            for copy in kv_copies(r):
-                copy.wait()
+            kv_copies(r)[0].wait()
         for r in pair_of:
             live_ctx = jnp.minimum(ctx_s[t * REQ + r] - s * WIDTH, WIDTH)
             live_new = new_s[t * REQ + r] - s * SHARE + WIDTH
@@ -267,7 +267,19 @@
     for load in loads[:3]:
         load.wait()
     stats = jnp.zeros((KVH * GROUP, 128), jnp.float32)
+    for r in range(2):
+        kv_copies(r)[1].wait()
     stats = attend((0, 1), stats)
+    slot = lax.broadcasted_iota(jnp.int32, (SHARE, 256), 0)
+    for r in range(2, REQ):
+        kv_copies(r)[1].wait()
+    for r in range(REQ):
+        live = slot < new_s[t * REQ + r] - s * SHARE
+        for h in range(KVH):
+            got[r, h, pl.ds(pl.multiple_of(s * SHARE, SHARE), SHARE), :] = jnp.where(
+                live, kv[r, h, WIDTH:, :], jnp.zeros((), jnp.bfloat16)
+            )
+
     pl.semaphore_wait(barrier, 37)
     drains.append(drain_o)
     send_o(0)
@@ -281,14 +293,6 @@
     for h in range(KVH):
         osend[h, 64:80, :] = pieces[h * GROUP:(h + 1) * GROUP]
     send_o(1)
-
-    slot = lax.broadcasted_iota(jnp.int32, (SHARE, 256), 0)
-    for r in range(REQ):
-        live = slot < new_s[t * REQ + r] - s * SHARE
-        for h in range(KVH):
-            got[r, h, pl.ds(pl.multiple_of(s * SHARE, SHARE), SHARE), :] = jnp.where(
-                live, kv[r, h, WIDTH:, :], jnp.zeros((), jnp.bfloat16)
-            )
 
     start_first(0, 1, 2)
     for n in range(REQ):
@@ -462,8 +466,8 @@
                 send_r2(way, part, k)
         if turn == 3:
             add_e()
-
-    start_second(0, 1)
+            start_second(0, 1)
+
 
     for load in loads[3:]:
         load.wait()
@@ -514,7 +518,7 @@
     drain_n()
 
 
-def step(queries, cache_kv, new_kv, ctx_len, new_len, wo, hidden_in, norm_gain):
+def step(queries, cache_kv, new_kv, ctx_len, new_len, owner, wo, hidden_in, norm_gain):
     bf, f32 = jnp.bfloat16, jnp.float32
     dma = pltpu.SemaphoreType.DMA
     anywhere = pl.BlockSpec(memory_space=pl.ANY)
@@ -526,9 +530,10 @@
             V((64, 128), bf),
             V((64, 128), bf),
             V((REQ, KVH, WIDTH, 256), bf),
+            pltpu.SMEM((64,), jnp.int32),
         ),
-        in_specs=[anywhere] * 8,
-        out_specs=(vmem, vmem, vmem),
+        in_specs=[anywhere] * 9,
+        out_specs=(vmem, vmem, vmem, pl.BlockSpec(memory_space=pltpu.SMEM)),
         scratch_shapes=[
             pltpu.SMEM((64,), jnp.int32), pltpu.SMEM((64,), jnp.int32),
             V((REQ, KVH, GROUP, HD), bf),
@@ -544,7 +549,7 @@
             V((4, 4, 24, 128), bf), V((4, 4, 24, 128), bf), V((4, 4, 16, 128), bf),
             V((1, 128), f32), V((128, 1, 128), f32),
             V((64, 128), f32),
-            dma((5,)), dma((REQ, 2)), dma((4,)), dma((4,)), dma((4,)),
+            dma((6,)), dma((REQ, 2)), dma((4,)), dma((4,)), dma((4,)),
             dma((2,)), dma((2,)), dma((1,)), dma((1,)),
             dma((2, 3, 4)), dma((2, 3, 4)), dma((3,)), dma((3,)), dma((3,)), dma((3,)), dma((1,)), dma((1,)),
             dma((2, 6)), dma((2, 6)), dma((2, 10)), dma((2, 10)),
@@ -556,14 +561,14 @@
     )(
         *(
             pltpu.with_memory_space_constraint(v, pltpu.HBM)
-            for v in (ctx_len, new_len, queries, cache_kv, new_kv, wo, hidden_in, norm_gain.reshape(1, 128))
+            for v in (owner, ctx_len, new_len, queries, cache_kv, new_kv, wo, hidden_in, norm_gain.reshape(1, 128))
         )
     )
 
 
 def store_kernel(
-    owner_hbm, res_in, norm_in, deliv_ref, res_hbm, norm_hbm, app_hbm,
-    owner_ref, zeros, out_sem, sem,
+    owner_ref, res_in, norm_in, deliv_ref, res_hbm, norm_hbm, app_hbm,
+    zeros, out_sem, sem,
 ):
     s = lax.axis_index("seq")
     t = lax.axis_index("tp")
@@ -578,8 +583,6 @@
     def mine(r):
         return owner_ref[t * REQ + r] == s
 
-    who = pltpu.make_async_copy(owner_hbm, owner_ref, sem.at[2])
-    who.start()
     small = (
         pltpu.make_async_copy(res_in, res_hbm, sem.at[0]),
         pltpu.make_async_copy(norm_in, norm_hbm, sem.at[1]),
@@ -587,7 +590,6 @@
     for copy in small:
         copy.start()
     zeros[...] = jnp.zeros_like(zeros)
-    who.wait()
     for r in range(REQ):
         @pl.when(mine(r))
         def _():
@@ -613,25 +615,24 @@
     return pl.pallas_call(
         store_kernel,
         out_shape=tuple(jax.ShapeDtypeStruct(v.shape, v.dtype) for v in (residual_out, normed, delivered)),
-        in_specs=[anywhere] + [vmem] * 3,
+        in_specs=[pl.BlockSpec(memory_space=pltpu.SMEM)] + [vmem] * 3,
         out_specs=(anywhere,) * 3,
         scratch_shapes=[
-            pltpu.SMEM((64,), jnp.int32),
             pltpu.VMEM((2, WIDTH, 256), jnp.bfloat16),
             pltpu.SemaphoreType.DMA((REQ, 4)),
-            pltpu.SemaphoreType.DMA((3,)),
+            pltpu.SemaphoreType.DMA((2,)),
         ],
         compiler_params=pltpu.CompilerParams(vmem_limit_bytes=20 * 1024 * 1024),
         cost_estimate=pl.CostEstimate(flops=0, bytes_accessed=6_000_000, transcendentals=0),
     )(
-        owner,
+        pltpu.with_memory_space_constraint(owner, pltpu.SMEM),
         *(pltpu.with_memory_space_constraint(v, pltpu.VMEM) for v in (residual_out, normed, delivered)),
     )
 
 
 def per_device(queries, cache_kv, new_kv, ctx_len, new_len, owner, wo, hidden_in, norm_gain):
-    residual_out, normed, delivered = step(
-        queries, cache_kv, new_kv, ctx_len, new_len, wo, hidden_in, norm_gain
+    residual_out, normed, delivered, owner = step(
+        queries, cache_kv, new_kv, ctx_len, new_len, owner, wo, hidden_in, norm_gain
     )
     return store(owner, residual_out, normed, delivered)
 

time: 42.8 us -> 42.3 us (0.988)
  Pallas kernels: 42 us -> 41.5 us
    pallas_call x1, Pallas kernels: 2.7 us -> 2.18 us  [store(): pl.pallas_call(store_kernel, out_shape=tuple((jax.ShapeDtypeStruct(v.shap...]
where the time goes in v8:
time: 42.3 us; the launch traced here: 42.2 us
  Pallas kernels  41.5 us (98%)
  between operations  0.64 us (2%)
    pallas_call x1, Pallas kernels, step(): pl.pallas_call(kernel, out_shape=(V((64, 128), bf), V((64, 128), bf), V((...  39.3 us
    pallas_call x1, Pallas kernels, store(): pl.pallas_call(store_kernel, out_shape=tuple((jax.ShapeDtypeStruct(v.shap...  2.18 us

profile of v8, /device:TPU:1, one launch (start us, length us, event | category | flops | bytes accessed | tf_op | source)
XLA Modules:
  0.0 42.2 jit_solution(17207469292394308036)
XLA Ops:
  0.6 39.3 %shard_map.112 = (bf16[64,128]{1,0:T(8,128)(2,1)S(1)}, bf16[64,128]{1,0:T(8,128)(2,1)S(1)}, bf16[4,8,256,256]{3,2,1,0:T(8,128)(2,1)S(1)}, s32[64]{0:T(128)S(4)}) custom-call(s32[64]{0:T(128)} %owner_hbm.1, s32[64]{0:T(128)} %ctx_hbm.1, s32[64]{0:T(128)} %new_hbm.1, bf16[4,8,16,128]{3,2,1,0:T(8,128)(2,1)} %q_hbm.1, bf16[4,8,256,256]{3,2,1,0:T(8,128)(2,1)} %cache_hbm.1, ...), custom_call_target="tpu_custom_call" | custom-call | flops 600000000 | bytes 14000000 | tf_op jit(solution)/shard_map/pallas_call | solution.py:527
  40.0 2.2 %shard_map.113 = (bf16[64,128]{1,0:T(8,128)(2,1)}, bf16[64,128]{1,0:T(8,128)(2,1)}, bf16[4,8,256,256]{3,2,1,0:T(8,128)(2,1)}) custom-call(s32[64]{0:T(128)S(4)} %get-tuple-element.7.owner_ref, bf16[64,128]{1,0:T(8,128)(2,1)S(1)} %get-tuple-element.8.res_in, bf16[64,128]{1,0:T(8,128)(2,1)S(1)} %get-tuple-element.9.norm_in, ...), custom_call_target="tpu_custom_call" | custom-call | bytes 6000000 | tf_op jit(solution)/shard_map/pallas_call | solution.py:615

commit v9 on v8

--- a/solution.py
+++ b/solution.py
@@ -27,7 +27,7 @@
 
 
 def kernel(
-    owner_hbm, ctx_hbm, new_hbm, q_hbm, cache_hbm, newkv_hbm, wo_hbm, hidden_hbm, gain_hbm,
+    after_hbm, owner_hbm, ctx_hbm, new_hbm, q_hbm, cache_hbm, newkv_hbm, wo_hbm, hidden_hbm, gain_hbm,
     res_ref, norm_ref, got, owner_out,
     ctx_s, new_s, q_v, kv, w_v, hid_v, gain_v,
     osend, orecv, csend, crecv,
@@ -416,17 +416,13 @@
             device = (j * 2 + c, x * 4 + k if way == 0 else k * 4 + z)
         return remote(send.at[j, k], recv.at[slot], r2s_sem.at[way], r2r_sem.at[way], device)
 
-    def send_r2(way, j, k):
+    def send_r2(way, dj, dk):
         send, recv = ((a2_send, a2_recv), (b2_send, b2_recv), (e2_send, e2_recv))[way]
         mine = ((y, z), (y, x), (x, z))[way]
-        away = (j != mine[0]) | (k != mine[1])
-
-        @pl.when(away)
-        def _():
+        j, k = (mine[0] + dj) & 3, (mine[1] + dk) & 3
+        if dj or dk:
             r2_copy(way, j, k).start()
-
-        @pl.when(jnp.logical_not(away))
-        def _():
+        else:
             pltpu.make_async_copy(send.at[j, k], recv.at[j, k], r2r_sem.at[way]).start()
 
     def drain_r2():
@@ -446,8 +442,9 @@
             out = out.astype(jnp.bfloat16)
             for k in range(4):
                 e2_send[j, k] = out[:, k * 128:(k + 1) * 128]
-            for k in range(4):
-                send_r2(2, j, k)
+        for dj in (2, 1, 3, 0):
+            for dk in (2, 1, 3, 0):
+                send_r2(2, dj, dk)
 
     drains.append(drain_r2)
     for turn in turns:
@@ -462,8 +459,8 @@
             out = out.astype(jnp.bfloat16)
             for k in range(4):
                 nxt[part, k] = out[:, k * 128:(k + 1) * 128]
-            for k in range(4):
-                send_r2(way, part, k)
+            for dk in (2, 1, 3, 0):
+                send_r2(way, turn, dk)
         if turn == 3:
             add_e()
             start_second(0, 1)
@@ -518,7 +515,7 @@
     drain_n()
 
 
-def step(queries, cache_kv, new_kv, ctx_len, new_len, owner, wo, hidden_in, norm_gain):
+def step(after, queries, cache_kv, new_kv, ctx_len, new_len, owner, wo, hidden_in, norm_gain):
     bf, f32 = jnp.bfloat16, jnp.float32
     dma = pltpu.SemaphoreType.DMA
     anywhere = pl.BlockSpec(memory_space=pl.ANY)
@@ -532,7 +529,7 @@
             V((REQ, KVH, WIDTH, 256), bf),
             pltpu.SMEM((64,), jnp.int32),
         ),
-        in_specs=[anywhere] * 9,
+        in_specs=[anywhere] * 10,
         out_specs=(vmem, vmem, vmem, pl.BlockSpec(memory_space=pltpu.SMEM)),
         scratch_shapes=[
             pltpu.SMEM((64,), jnp.int32), pltpu.SMEM((64,), jnp.int32),
@@ -561,13 +558,43 @@
     )(
         *(
             pltpu.with_memory_space_constraint(v, pltpu.HBM)
-            for v in (owner, ctx_len, new_len, queries, cache_kv, new_kv, wo, hidden_in, norm_gain.reshape(1, 128))
+            for v in (after, owner, ctx_len, new_len, queries, cache_kv, new_kv, wo, hidden_in, norm_gain.reshape(1, 128))
         )
     )
 
 
+def starts_early():
+    return (lax.axis_index("tp") & 3) == 0
+
+
+def blank_kernel(app_hbm, zeros, sem):
+    def blank(r, i):
+        return pltpu.make_async_copy(zeros, app_hbm.at[r, pl.ds(i * 2, 2)], sem.at[r, i])
+
+    @pl.when(starts_early())
+    def _():
+        zeros[...] = jnp.zeros_like(zeros)
+        for r in range(REQ):
+            for i in range(4):
+                blank(r, i).start()
+        for r in range(REQ):
+            for i in range(4):
+                blank(r, i).wait()
+
+
+def blanks():
+    return pl.pallas_call(
+        blank_kernel,
+        out_shape=pltpu.HBM((REQ, KVH, WIDTH, 256), jnp.bfloat16),
+        out_specs=pl.BlockSpec(memory_space=pl.ANY),
+        scratch_shapes=[pltpu.VMEM((2, WIDTH, 256), jnp.bfloat16), pltpu.SemaphoreType.DMA((REQ, 4))],
+        compiler_params=pltpu.CompilerParams(vmem_limit_bytes=20 * 1024 * 1024),
+        cost_estimate=pl.CostEstimate(flops=0, bytes_accessed=4_000_000, transcendentals=0),
+    )()
+
+
 def store_kernel(
-    owner_ref, res_in, norm_in, deliv_ref, res_hbm, norm_hbm, app_hbm,
+    owner_ref, res_in, norm_in, deliv_ref, app_in, res_hbm, norm_hbm, app_hbm,
     zeros, out_sem, sem,
 ):
     s = lax.axis_index("seq")
@@ -589,7 +616,10 @@
     )
     for copy in small:
         copy.start()
-    zeros[...] = jnp.zeros_like(zeros)
+    @pl.when(jnp.logical_not(starts_early()))
+    def _():
+        zeros[...] = jnp.zeros_like(zeros)
+
     for r in range(REQ):
         @pl.when(mine(r))
         def _():
@@ -597,7 +627,7 @@
                 put(r, i).start()
 
     for r in range(REQ):
-        @pl.when(jnp.logical_not(mine(r)))
+        @pl.when(jnp.logical_not(mine(r) | starts_early()))
         def _():
             for i in range(4):
                 blank(r, i).start()
@@ -605,36 +635,41 @@
     for copy in small:
         copy.wait()
     for r in range(REQ):
-        for i in range(4):
-            put(r, i).wait()
-
-
-def store(owner, residual_out, normed, delivered):
+        @pl.when(mine(r) | jnp.logical_not(starts_early()))
+        def _():
+            for i in range(4):
+                put(r, i).wait()
+
+
+def store(owner, residual_out, normed, delivered, appended):
     anywhere = pl.BlockSpec(memory_space=pl.ANY)
     vmem = pl.BlockSpec(memory_space=pltpu.VMEM)
     return pl.pallas_call(
         store_kernel,
         out_shape=tuple(jax.ShapeDtypeStruct(v.shape, v.dtype) for v in (residual_out, normed, delivered)),
-        in_specs=[pl.BlockSpec(memory_space=pltpu.SMEM)] + [vmem] * 3,
+        in_specs=[pl.BlockSpec(memory_space=pltpu.SMEM)] + [vmem] * 3 + [anywhere],
         out_specs=(anywhere,) * 3,
         scratch_shapes=[
             pltpu.VMEM((2, WIDTH, 256), jnp.bfloat16),
             pltpu.SemaphoreType.DMA((REQ, 4)),
             pltpu.SemaphoreType.DMA((2,)),
         ],
+        input_output_aliases={4: 2},
         compiler_params=pltpu.CompilerParams(vmem_limit_bytes=20 * 1024 * 1024),
         cost_estimate=pl.CostEstimate(flops=0, bytes_accessed=6_000_000, transcendentals=0),
     )(
         pltpu.with_memory_space_constraint(owner, pltpu.SMEM),
         *(pltpu.with_memory_space_constraint(v, pltpu.VMEM) for v in (residual_out, normed, delivered)),
+        appended,
     )
 
 
 def per_device(queries, cache_kv, new_kv, ctx_len, new_len, owner, wo, hidden_in, norm_gain):
+    appended = blanks()
     residual_out, normed, delivered, owner = step(
-        queries, cache_kv, new_kv, ctx_len, new_len, owner, wo, hidden_in, norm_gain
+        appended, queries, cache_kv, new_kv, ctx_len, new_len, owner, wo, hidden_in, norm_gain
     )
-    return store(owner, residual_out, normed, delivered)
+    return store(owner, residual_out, normed, delivered, appended)
 
 
 def solution(mesh):

time: 42.3 us -> 41.7 us (0.986)
  Pallas kernels: 41.5 us -> 41 us
    pallas_call x0 -> x1, Pallas kernels: none -> 2.16 us  [blanks(): pl.pallas_call(blank_kernel, out_shape=pltpu.HBM((REQ, KVH, WIDTH, 256),...]
    pallas_call x1, Pallas kernels: 39.3 us -> 37.3 us  [step(): pl.pallas_call(kernel, out_shape=(V((64, 128), bf), V((64, 128), bf), V((...]
    pallas_call x1, Pallas kernels: 2.18 us -> 1.49 us  [store(): pl.pallas_call(store_kernel, out_shape=tuple((jax.ShapeDtypeStruct(v.shap...]
where the time goes in v9:
time: 41.7 us; the launch traced here: 41.6 us
  Pallas kernels  41 us (98%)
  between operations  0.65 us (2%)
    pallas_call x1, Pallas kernels, step(): pl.pallas_call(kernel, out_shape=(V((64, 128), bf), V((64, 128), bf), V((...  37.3 us
    pallas_call x1, Pallas kernels, blanks(): pl.pallas_call(blank_kernel, out_shape=pltpu.HBM((REQ, KVH, WIDTH, 256),...  2.16 us
    pallas_call x1, Pallas kernels, store(): pl.pallas_call(store_kernel, out_shape=tuple((jax.ShapeDtypeStruct(v.shap...  1.49 us

profile of v9, /device:TPU:1, one launch (start us, length us, event | category | flops | bytes accessed | tf_op | source)
XLA Modules:
  0.0 41.6 jit_solution(1643367463041327925)
XLA Ops:
  0.6 2.2 %shard_map.112.after_hbm.app_in = bf16[4,8,256,256]{3,2,1,0:T(8,128)(2,1)} custom-call(), custom_call_target="tpu_custom_call" | custom-call | bytes 4000000 | tf_op jit(solution)/shard_map/pallas_call | solution.py:586
  2.8 37.3 %shard_map.113 = (bf16[64,128]{1,0:T(8,128)(2,1)S(1)}, bf16[64,128]{1,0:T(8,128)(2,1)S(1)}, bf16[4,8,256,256]{3,2,1,0:T(8,128)(2,1)S(1)}, s32[64]{0:T(128)S(4)}) custom-call(bf16[4,8,256,256]{3,2,1,0:T(8,128)(2,1)} %shard_map.112.after_hbm.app_in, s32[64]{0:T(128)} %owner_hbm.1, s32[64]{0:T(128)} %ctx_hbm.1, s32[64]{0:T(128)} %new_hbm.1, ...), custom_call_target="tpu_custom_call" | custom-call | flops 600000000 | bytes 14000000 | tf_op jit(solution)/shard_map/pallas_call | solution.py:524
  40.1 1.5 %shard_map.114 = (bf16[64,128]{1,0:T(8,128)(2,1)}, bf16[64,128]{1,0:T(8,128)(2,1)}, bf16[4,8,256,256]{3,2,1,0:T(8,128)(2,1)}) custom-call(s32[64]{0:T(128)S(4)} %get-tuple-element.7.owner_ref, bf16[64,128]{1,0:T(8,128)(2,1)S(1)} %get-tuple-element.8.res_in, bf16[64,128]{1,0:T(8,128)(2,1)S(1)} %get-tuple-element.9.norm_in, ...), custom_call_target="tpu_custom_call", output_to_operand_aliasing={{2}: (4, {})} | custom-call | bytes 6000000 | tf_op jit(solution)/shard_map/pallas_call | solution.py:647

commit v10 on v9

--- a/solution.py
+++ b/solution.py
@@ -253,7 +253,8 @@
             o_copy(seq_peer(i), part).start()
             return 0
 
-        lax.fori_loop(0, 7, one, 0)
+        for i in range(7):
+            one(i, 0)
 
     def wait_o(part):
         everything = orecv.at[:, rows_of(part)]
@@ -349,7 +350,9 @@
             pltpu.make_async_copy(sent, sent, cs_sem.at[0]).wait()
 
     drains.append(drain_c)
-    others(16, 10, send_c)
+    for i in range(16):
+        if i != 10:
+            send_c(i, 0)
     c_copy(1 - c, t).start()
     pltpu.make_async_copy(csend.at[t], crecv.at[c, t], cr_sem.at[0]).start()
     for j in range(4):

time: 41.7 us -> 41 us (0.983)
  Pallas kernels: 41 us -> 40.3 us
    pallas_call x1, Pallas kernels: 1.49 us -> 0.78 us  [store(): pl.pallas_call(store_kernel, out_shape=tuple((jax.ShapeDtypeStruct(v.shap...]
where the time goes in v10:
time: 41 us; the launch traced here: 40.9 us
  Pallas kernels  40.3 us (98%)
  between operations  0.65 us (2%)
    pallas_call x1, Pallas kernels, step(): pl.pallas_call(kernel, out_shape=(V((64, 128), bf), V((64, 128), bf), V((...  37.4 us
    pallas_call x1, Pallas kernels, blanks(): pl.pallas_call(blank_kernel, out_shape=pltpu.HBM((REQ, KVH, WIDTH, 256),...  2.16 us

profile of v10, /device:TPU:1, one launch (start us, length us, event | category | flops | bytes accessed | tf_op | source)
XLA Modules:
  0.0 40.9 jit_solution(2622888921666650135)
XLA Ops:
  0.6 2.2 %shard_map.112.after_hbm.app_in = bf16[4,8,256,256]{3,2,1,0:T(8,128)(2,1)} custom-call(), custom_call_target="tpu_custom_call" | custom-call | bytes 4000000 | tf_op jit(solution)/shard_map/pallas_call | solution.py:589
  2.8 37.4 %shard_map.113 = (bf16[64,128]{1,0:T(8,128)(2,1)S(1)}, bf16[64,128]{1,0:T(8,128)(2,1)S(1)}, bf16[4,8,256,256]{3,2,1,0:T(8,128)(2,1)S(1)}, s32[64]{0:T(128)S(4)}) custom-call(bf16[4,8,256,256]{3,2,1,0:T(8,128)(2,1)} %shard_map.112.after_hbm.app_in, s32[64]{0:T(128)} %owner_hbm.1, s32[64]{0:T(128)} %ctx_hbm.1, s32[64]{0:T(128)} %new_hbm.1, ...), custom_call_target="tpu_custom_call" | custom-call | flops 600000000 | bytes 14000000 | tf_op jit(solution)/shard_map/pallas_call | solution.py:527
  40.2 0.8 %shard_map.114 = (bf16[64,128]{1,0:T(8,128)(2,1)}, bf16[64,128]{1,0:T(8,128)(2,1)}, bf16[4,8,256,256]{3,2,1,0:T(8,128)(2,1)}) custom-call(s32[64]{0:T(128)S(4)} %get-tuple-element.7.owner_ref, bf16[64,128]{1,0:T(8,128)(2,1)S(1)} %get-tuple-element.8.res_in, bf16[64,128]{1,0:T(8,128)(2,1)S(1)} %get-tuple-element.9.norm_in, ...), custom_call_target="tpu_custom_call", output_to_operand_aliasing={{2}: (4, {})} | custom-call | bytes 6000000 | tf_op jit(solution)/shard_map/pallas_call | solution.py:650
